TPU v7x, 256 devices: a whole 4x4x8 slice. The times are simulated.
256 devices in a mesh: row: 32 (over x, z_lo, core), col: 8 (over z_hi, y).
Axes of the slice: x: 4, y: 4, z: 8 (z_hi: 2, z_lo: 4; z = z_hi * 4 + z_lo), core: 2. Of those that a mesh axis runs over, the one named last changes fastest.
Arguments:
- s_band: bfloat16 [256, 65536], P(None, ('col', 'row')), may hold values from -6 to 6
- t_band: bfloat16 [256, 65536], P(None, ('col', 'row')), may hold values from -6 to 6
- q_rows: bfloat16 [4096, 65536], P('row', 'col'), may hold values from -6 to 6
- z_rows: bfloat16 [4096, 65536], P('row', 'col'), may hold values from -6 to 6
- factors: bfloat16 [16, 2, 256, 256], P(None, None, 'row', 'col'), may hold values from -0.375 to 0.375
- starts: int32 [16], replicated, may hold values from 0 to 65280, as said below
- flags: int32 [16], replicated, may hold values from 0 to 1, as said below
Outputs:
- q_out: bfloat16 [4096, 65536], P('row', 'col')
- z_out: bfloat16 [4096, 65536], P('row', 'col')
- s_out: bfloat16 [256, 65536], P(None, ('col', 'row'))
- t_out: bfloat16 [256, 65536], P(None, ('col', 'row'))
Inputs may be any that keep to these rules, and one draw needn't show every extreme that they name: The starts are distinct multiples of 256; starts[0] = 0. At most 8 windows start within the columns of one index of col, and exactly 8 do for some index. flags[0] = 1.
All inputs are finite; a program needn't handle non-finite values.
Results may differ from a plain program's by a relative error of at most 0.0013.
Values may be sent and summed in bfloat16 or wider, within the bound.
A program may use at most 64 MiB of HBM per device.

v0:
```python
import jax
import jax.numpy as jnp
from jax import lax
from jax.sharding import PartitionSpec as P

W = 256
K = 16


def take_blocks(matrix, places):
    return jax.vmap(lambda place: lax.dynamic_slice_in_dim(matrix, place, W, 1))(places)


def place_blocks(matrix, blocks, places, live):

    def write_one(slot, current_matrix):
        current = lax.dynamic_slice_in_dim(current_matrix, places[slot], W, 1)
        value = jnp.where(live[slot], blocks[slot], current)
        return lax.dynamic_update_slice_in_dim(current_matrix, value, places[slot], 1)

    return lax.fori_loop(0, places.shape[0], write_one, matrix)


def contribute(blocks, factor_piece):
    return jnp.einsum("srp,spw->srw", blocks, factor_piece, preferred_element_type=jnp.float32)


def local(s_band, t_band, q_rows, z_rows, factors, starts, flags):
    band_height, band_width = s_band.shape
    q_height, width_local = q_rows.shape
    n_row = lax.axis_size("row")
    column = lax.axis_index("col")
    row_place = lax.axis_index("row")
    offset = starts - column * width_local
    owned = (offset >= 0) & (offset < width_local) & (flags == 1)
    band_offset = starts - (column * n_row + row_place) * band_width
    band_owned = (band_offset >= 0) & (band_offset < band_width) & (flags == 1)
    slots = jnp.arange(K, dtype=jnp.int32)
    band_slots = jnp.arange(K, dtype=jnp.int32)
    live = owned[slots]
    places = jnp.clip(offset[slots], 0, width_local - W)
    band_live = band_owned[band_slots]
    band_places = jnp.clip(band_offset[band_slots], 0, band_width - W)
    left_blocks = take_blocks(q_rows, places)
    right_blocks = take_blocks(z_rows, places)
    band_blocks = jnp.concatenate(
        [take_blocks(s_band, band_places), take_blocks(t_band, band_places)], axis=1
    )
    factor_cols = lax.all_gather(factors, "col", axis=3, tiled=True)
    piece = lax.all_gather(factor_cols, "row", axis=2, tiled=True)
    picked = jnp.take(piece, slots, axis=0)
    band_picked = jnp.take(piece[:, 1], band_slots, axis=0)
    acc_left = contribute(left_blocks, picked[:, 0])
    acc_right = contribute(right_blocks, picked[:, 1])
    acc_band = contribute(band_blocks, band_picked)
    leading = piece[0, 0]
    acc_left, acc_right, acc_band, leading = (acc_left, acc_right, acc_band, leading)
    q_out = place_blocks(q_rows, acc_left.astype(q_rows.dtype), places, live)
    z_out = place_blocks(z_rows, acc_right.astype(z_rows.dtype), places, live)
    fresh_band = acc_band.astype(s_band.dtype)
    s_mid = place_blocks(s_band, fresh_band[:, :band_height], band_places, band_live)
    t_mid = place_blocks(t_band, fresh_band[:, band_height:], band_places, band_live)
    s_out = lax.dot_general(
        leading, s_mid, (((0,), (0,)), ((), ())), preferred_element_type=jnp.float32
    ).astype(s_band.dtype)
    t_out = lax.dot_general(
        leading, t_mid, (((0,), (0,)), ((), ())), preferred_element_type=jnp.float32
    ).astype(t_band.dtype)
    return (q_out, z_out, s_out, t_out)


def solution(mesh):
    in_specs = (
        P(None, ("col", "row")),
        P(None, ("col", "row")),
        P("row", "col"),
        P("row", "col"),
        P(None, None, "row", "col"),
        P(),
        P(),
    )
    out_specs = (P("row", "col"), P("row", "col"), P(None, ("col", "row")), P(None, ("col", "row")))
    return jax.shard_map(local, mesh=mesh, in_specs=in_specs, out_specs=out_specs, check_vma=False)
```

profile of v0, /device:TPU:218, one launch (start us, length us, event | category | flops | bytes accessed | tf_op | source)
XLA Modules:
  0.0 426.7 jit_solution(4903666067037326566)
XLA Ops:
  7.2 3.2 copy.69
  12.0 48.3 %all_gather.6 = bf16[16,2,8,256]{0,2,1,3:T(8,128)(2,1)S(1)} all-gather(bf16[16,2,8,32]{0,2,1,3:T(8,128)(2,1)S(1)} %copy.16), channel_id=1, replica_groups=mesh['row'=32,'col'=8] {'col'}, dimensions={3}, use_global_device_ids=true | all-gather | bytes 147456 | tf_op jit(solution)/shard_map/all_gather | solution.py:49
  64.2 36.7 %while.59 = (s32[]{:T(128)}, bf16[128,8192]{1,0:T(8,128)(2,1)}, s32[16,2]{0,1:T(2,128)S(1)}, bf16[16,128,256]{2,1,0:T(8,128)(2,1)S(1)}, s32[]{:T(128)}) while((s32[]{:T(128)}, bf16[128,8192]{1,0:T(8,128)(2,1)}, s32[16,2]{0,1:T(2,128)S(1)}, bf16[16,128,256]{2,1,0:T(8,128)(2,1)S(1)}, s32[]{:T(128)}) %tuple.135), condition=%wide.while_cond.1, body=%wide.while_body.1.sunk | while | flops 2 | bytes 131169 | solution.py:11
  101.0 36.1 %while.58 = (s32[]{:T(128)}, bf16[128,8192]{1,0:T(8,128)(2,1)}, s32[16,2]{0,1:T(2,128)S(1)}, bf16[16,128,256]{2,1,0:T(8,128)(2,1)S(1)}, s32[]{:T(128)}) while((s32[]{:T(128)}, bf16[128,8192]{1,0:T(8,128)(2,1)}, s32[16,2]{0,1:T(2,128)S(1)}, bf16[16,128,256]{2,1,0:T(8,128)(2,1)S(1)}, s32[]{:T(128)}) %tuple.150), condition=%wide.while_cond, body=%wide.while_body.sunk | while | flops 2 | bytes 131169 | solution.py:11
  112.9 1.6 bitcast_dynamic-update-slice_fusion.4
  137.0 5.0 %gather_fusion.2 = bf16[16,2,256,256]{3,2,1,0:T(8,128)(2,1)} fusion(bf16[16,2,256,256]{3,2,1,0:T(8,128)(2,1)} %all-gather.2.cloned.1.call-done, s32[1024]{0:T(1024)S(1)} %pad_clamp_fusion), kind=kCustom, calls=%fused_computation.2 | custom fusion | bytes 8388672 | tf_op jit(solution)/shard_map/jit(_take)/gather | solution.py:51
  142.0 2.6 copy_select_fusion
  146.7 101.4 %while.55 = (s32[]{:T(128)}, bf16[128,8192]{1,0:T(8,128)(2,1)}, pred[16]{0:T(512)(128)(4,1)S(1)}, bf16[16,128,256]{2,1,0:T(8,128)(2,1)S(1)}, s32[16]{0:T(128)S(1)}, /*index=5*/s32[]{:T(128)}, s32[]{:T(128)}, s32[]{:T(128)}) while((s32[]{:T(128)}, bf16[128,8192]{1,0:T(8,128)(2,1)}, pred[16]{0:T(512)(128)(4,1)S(1)}, ...), condition=%wide.region_3.4_spmd, body=%wide.region_2.3_spmd.sunk | while | flops 32773 | bytes 327830 | solution.py:21
  149.8 1.6 bitcast_select_fusion.9
  156.1 1.6 bitcast_select_fusion.9
  162.5 1.6 bitcast_select_fusion.9
  168.8 1.6 bitcast_select_fusion.9
  175.2 1.6 bitcast_select_fusion.9
  181.5 1.6 bitcast_select_fusion.9
  213.2 1.6 bitcast_select_fusion.9
  248.1 2.0 fusion.11
  250.1 101.4 %while.54 = (s32[]{:T(128)}, bf16[128,8192]{1,0:T(8,128)(2,1)}, pred[16]{0:T(512)(128)(4,1)S(1)}, bf16[16,128,256]{2,1,0:T(8,128)(2,1)S(1)}, s32[16]{0:T(128)S(1)}, /*index=5*/s32[]{:T(128)}, s32[]{:T(128)}, s32[]{:T(128)}) while((s32[]{:T(128)}, bf16[128,8192]{1,0:T(8,128)(2,1)}, pred[16]{0:T(512)(128)(4,1)S(1)}, ...), condition=%wide.region_1.2_spmd, body=%wide.region_0.1_spmd.sunk | while | flops 32773 | bytes 327830 | solution.py:21
  329.4 1.6 bitcast_select_fusion.8
  342.1 1.6 bitcast_select_fusion.8
  351.5 1.7 slice_bitcast_fusion
  353.3 2.0 gather_fusion.4
  358.5 1.7 fusion.18
  360.2 35.1 %while.56 = (s32[]{:T(128)}, bf16[256,256]{1,0:T(8,128)(2,1)S(1)}, pred[16]{0:T(512)(128)(4,1)S(1)}, bf16[16,256,256]{2,1,0:T(8,128)(2,1)}, s32[]{:T(128)}) while((s32[]{:T(128)}, bf16[256,256]{1,0:T(8,128)(2,1)S(1)}, pred[16]{0:T(512)(128)(4,1)S(1)}, bf16[16,256,256]{2,1,0:T(8,128)(2,1)}, s32[]{:T(128)}) %tuple.141), condition=%wide.region_5.6_spmd, body=%wide.region_4.5_spmd.sunk | while | flops 65538 | bytes 393288 | solution.py:21
  397.2 20.7 %while.57 = (s32[]{:T(128)}, bf16[256,256]{1,0:T(8,128)(2,1)S(1)}, pred[16]{0:T(512)(128)(4,1)S(1)}, bf16[16,256,256]{2,1,0:T(8,128)(2,1)S(1)}, s32[]{:T(128)}) while((s32[]{:T(128)}, bf16[256,256]{1,0:T(8,128)(2,1)S(1)}, pred[16]{0:T(512)(128)(4,1)S(1)}, bf16[16,256,256]{2,1,0:T(8,128)(2,1)S(1)}, s32[]{:T(128)}) %tuple.151), condition=%wide.region_7.8_spmd, body=%wide.region_6.7_spmd.sunk | while | flops 65538 | bytes 393288 | solution.py:21
  (322 shorter events, 265.7 us)
Async XLA Ops:
  7.2 3.3 copy-start.1
  7.2 129.9 %all-gather.2.cloned.1.call-start = ((), (), s32[]{:S(2)}) async-start(), calls=%async_computation | async-start | bytes 4325376 | tf_op jit(solution)/shard_map/all_gather | solution.py:50
  10.5 1.3 copy-start.3
  10.5 1.4 copy-start.4
  10.5 1.4 copy-start.5
  11.8 50.2 %copy-start.6 = (s32[16]{0:T(128)S(1)}, s32[16]{0:T(128)}, u32[]{:S(2)}) copy-start(s32[16]{0:T(128)} %param.21) | copy-start | bytes 196
  11.8 50.2 %copy-start.7 = (s32[16]{0:T(128)S(1)}, s32[16]{0:T(128)}, u32[]{:S(2)}) copy-start(s32[16]{0:T(128)} %param.20) | copy-start | bytes 196
  144.7 2.0 copy-start
  355.3 1.6 copy-start.2
Sparse Core Ops, SparseCore 0:
  62.1 69.0 all-gather.1
where the time goes:
time: 433 us; the launch traced here: 427 us
  local copies, waits for them, and re-layouts  203 us (47%)
  other arithmetic  91.2 us (21%)
  loops' own time  63.7 us (15%)
  blocking collectives  48.3 us (11%)
  between operations  14.3 us (3%)
  matrix products  6.33 us (1%)
    select_n x64, other arithmetic, write_one(): value = jnp.where(live[slot], blocks[slot], current)  88.5 us
    gather x96, local copies, waits for them, and re-layouts  72.1 us
    another operation x4, loops' own time, place_blocks(): return lax.fori_loop(0, places.shape[0], write_one, matrix)  63 us
    dynamic_update_slice x32, local copies, waits for them, and re-layouts, write_one(): lax.dynamic_update_slice_in_dim(current_matrix, value, places[slot], 1)  50.7 us
    all_gather x1, blocking collectives, local(): factor_cols = lax.all_gather(factors, 'col', axis=3, tiled=True)  48.3 us
    dynamic_slice x64, local copies, waits for them, and re-layouts, write_one(): value = jnp.where(live[slot], blocks[slot], current)  37.7 us
    dynamic_slice x32, local copies, waits for them, and re-layouts, write_one(): current = lax.dynamic_slice_in_dim(current_matrix, places[slot], W, 1)  18.6 us
    unnamed x25, local copies, waits for them, and re-layouts  9.2 us
  transfers between devices with their start and end apart: 1, of which 0 were waited for; matrix products, arithmetic and copies ran while one was open for 17% of the time, Pallas kernels for 0%

commit v1 on v0

v1 whole, which is shorter than its diff:
```python
import jax
import jax.numpy as jnp
from jax import lax
from jax.experimental import pallas as pl
from jax.experimental.pallas import tpu as pltpu
from jax.sharding import PartitionSpec as P

W = 256
K = 16
SLOTS = 8
UNITS = 2 * SLOTS + 1
ROWS = 32
COLS = 8
TILES = 32
HALF = 9
BF = jnp.bfloat16
F32 = jnp.float32


def slot_words(starts_ref, column):
    word = jnp.int32(0)
    for k in reversed(range(K)):
        mine = (starts_ref[k] >> 13) == column
        word = jnp.where(mine, (word << 4) | k, word)
    return word


def remote(src, dst, send_sem, recv_sem, device):
    return pltpu.make_async_remote_copy(
        src_ref=src,
        dst_ref=dst,
        send_sem=send_sem,
        recv_sem=recv_sem,
        device_id=device,
        device_id_type=pl.DeviceIdType.MESH,
    )


def gather_kernel(
    starts_hbm, factors_hbm, q_hbm, z_hbm, s_hbm, t_hbm,
    g_ref, qv, zv, sv, tv,
    starts_ref, fac, wide, send1, recv1, send0, recv0,
    load_sem, ss1, rs1, ss0, rs0, sz, rz, sxp, rxp, sxm, rxm, sop, rop, som, rom, ssib, rsib,
):
    r = lax.axis_index("row")
    c = lax.axis_index("col")
    core = r % 2
    x = r // 8
    zl = (r // 2) % 4
    me = core * 8 + c
    xp = (r + 8) % ROWS
    xm = (r + ROWS - 8) % ROWS
    sib = r + 1 - 2 * core
    base = r - core

    barrier = pltpu.get_barrier_semaphore()

    def greet(device):
        pl.semaphore_signal(barrier, inc=1, device_id=device, device_id_type=pl.DeviceIdType.MESH)

    loads = [
        pltpu.make_async_copy(a, b, load_sem.at[i])
        for i, (a, b) in enumerate(
            [(factors_hbm, fac), (starts_hbm, starts_ref), (q_hbm, qv), (z_hbm, zv), (s_hbm, sv), (t_hbm, tv)]
        )
    ]
    loads[0].start()
    loads[1].start()
    for k in range(1, 16):
        other = (me + k) % 16
        greet((base + other // 8, other % 8))
    greet((xp, c))
    greet((xm, c))

    @pl.when(zl < 3)
    def _():
        greet((r + 2, c))

    @pl.when(zl > 0)
    def _():
        greet((r - 2, c))

    wide[...] = jnp.zeros_like(wide)
    loads[0].wait()
    loads[1].wait()
    for load in loads[2:]:
        load.start()
    for k in range(K):
        for m in range(2):
            wide[k, 8 * m : 8 * m + 8, 0:32] = fac[k, m].astype(F32)
    for dest in range(COLS):
        word = slot_words(starts_ref, dest)
        rows = []
        for a in range(2):
            total = None
            for b in range(4):
                k = (word >> (4 * (4 * a + b))) & 15
                piece = wide[k]
                if b:
                    piece = pltpu.roll(piece, 32 * b, 1)
                total = piece if total is None else total + piece
            rows.append(total)
        for m in range(2):
            send1[m * 8 + dest] = jnp.concatenate(
                [rows[0][8 * m : 8 * m + 8], rows[1][8 * m : 8 * m + 8]], axis=0
            ).astype(BF)
    lead = wide[0, 0:8]
    placed = lead
    for b in range(1, 4):
        placed = jnp.where(c % 4 == b, pltpu.roll(lead, 32 * b, 1), placed)
    nothing = jnp.zeros_like(placed)
    send0[...] = jnp.concatenate(
        [jnp.where(core == 0, placed, nothing), jnp.where(core == 1, placed, nothing)], axis=0
    ).astype(BF)

    pl.semaphore_wait(
        barrier, 17 + jnp.where(zl < 3, 1, 0) + jnp.where(zl > 0, 1, 0)
    )

    first = []
    for k in range(1, 16):
        other = (me + k) % 16
        copy = remote(send1.at[other], recv1.at[me], ss1.at[k], rs1.at[me], (base + other // 8, other % 8))
        copy.start()
        first.append(copy)
    half = c // 4
    mine0 = core * 4 + c % 4
    lead_copies = []
    for k in range(COLS):
        dest = (c + k) % COLS
        copy = remote(send0, recv0.at[mine0], ss0.at[k], rs0.at[mine0], (base + half, dest))
        if k == 0:
            pl.when(half != core)(copy.start)
        else:
            copy.start()
        lead_copies.append(copy)
    recv1[me] = send1[me]

    @pl.when(half == core)
    def _():
        recv0[mine0] = send0[...]

    for k in range(1, 16):
        other = (me + k) % 16
        remote(recv1.at[other], recv1.at[other], ss1.at[k], rs1.at[other], (sib, c)).wait_recv()
    for k in range(8):
        wait = remote(recv0.at[k], recv0.at[k], ss0.at[0], rs0.at[k], (sib, c)).wait_recv
        pl.when(jnp.logical_or(half != core, k != mine0))(wait)

    lane = lax.broadcasted_iota(jnp.int32, (16, 128), 1) // 32
    for h in range(2):
        turned = {}
        for s in range(2):
            for cc in range(4):
                piece = recv1[s * 8 + 4 * h + cc].astype(F32)
                for turn in range(4):
                    turned[s, cc, turn] = pltpu.roll(piece, 32 * turn, 1) if turn else piece
        for b in range(4):
            joined = []
            for s in range(2):
                out = turned[s, 0, (0 - b) % 4]
                for cc in range(1, 4):
                    out = jnp.where(lane == cc, turned[s, cc, (cc - b) % 4], out)
                joined.append(out)
            for a in range(2):
                g_ref[r, 2 * (4 * a + b) + h] = jnp.concatenate(
                    [joined[0][8 * a : 8 * a + 8], joined[1][8 * a : 8 * a + 8]], axis=0
                ).astype(BF)
    total = recv0[0].astype(F32)
    for k in range(1, 8):
        total = total + recv0[k].astype(F32)
    g_ref[r, 2 * SLOTS] = total.astype(BF)

    order = [
        zl,
        jnp.where(zl == 0, 1, jnp.where(zl == 1, 0, jnp.where(zl == 2, 1, 2))),
        jnp.where(zl < 2, 2, jnp.where(zl == 2, 3, 1)),
        jnp.where(zl < 2, 3, 0),
    ]

    def block(xx, zz):
        return ((xx + 4) % 4) * 8 + zz * 2 + core

    def to_sibling(ref, n):
        remote(ref, ref, ssib.at[n], rsib.at[n], (sib, c)).start()

    lo = pl.ds(0, HALF)
    hi = pl.ds(HALF, UNITS - HALF)

    def opposite(i, start):
        zz = order[i]
        b = block(x + 2, zz)
        remote(g_ref.at[b, lo], g_ref.at[b, lo], sop.at[zz], rop.at[zz], (sib, c)).wait_recv()
        to_sibling(g_ref.at[b, lo], 12 + zz)
        remote(g_ref.at[b, hi], g_ref.at[b, hi], som.at[zz], rom.at[zz], (sib, c)).wait_recv()
        to_sibling(g_ref.at[b, hi], 16 + zz)

    ups, downs = [], []
    for i in range(4):
        zz = order[i]
        own = g_ref.at[block(x, zz)]
        if i:
            remote(own, own, sz.at[0], rz.at[zz], (sib, c)).wait_recv()
        up = remote(own, own, sz.at[zz], rz.at[zz], (r + 2, c))
        down = remote(own, own, sz.at[4 + zz], rz.at[zz], (r - 2, c))
        goes_up = jnp.logical_and(zz <= zl, zl < 3)
        goes_down = jnp.logical_and(zz >= zl, zl > 0)
        pl.when(goes_up)(up.start)
        pl.when(goes_down)(down.start)
        ups.append((goes_up, up))
        downs.append((goes_down, down))
        remote(own, own, sxp.at[zz], rxp.at[zz], (xp, c)).start()
        remote(own, own, sxm.at[zz], rxm.at[zz], (xm, c)).start()
        to_sibling(own, zz)
        b = block(x - 1, zz)
        remote(g_ref.at[b], g_ref.at[b], sxp.at[zz], rxp.at[zz], (sib, c)).wait_recv()
        remote(g_ref.at[b, lo], g_ref.at[b, lo], sop.at[zz], rop.at[zz], (xp, c)).start()
        to_sibling(g_ref.at[b], 4 + zz)
        b = block(x + 1, zz)
        remote(g_ref.at[b], g_ref.at[b], sxm.at[zz], rxm.at[zz], (sib, c)).wait_recv()
        remote(g_ref.at[b, hi], g_ref.at[b, hi], som.at[zz], rom.at[zz], (xm, c)).start()
        to_sibling(g_ref.at[b], 8 + zz)
        if i:
            opposite(i - 1, False)
    opposite(3, False)

    theirs = 1 - core
    for n in range(20):
        if n < 12:
            b = ((x + (0, 3, 1)[n // 4]) % 4) * 8 + (n % 4) * 2 + theirs
            ref = g_ref.at[b]
        else:
            b = ((x + 2) % 4) * 8 + (n % 4) * 2 + theirs
            ref = g_ref.at[b, lo if n < 16 else hi]
        remote(ref, ref, ssib.at[n], rsib.at[n], (sib, c)).wait_recv()
        remote(ref, ref, ssib.at[n], rsib.at[n], (sib, c)).wait_send()
    for goes, copy in ups + downs:
        pl.when(goes)(copy.wait_send)
    for zz in range(4):
        ref = g_ref.at[0]
        remote(ref, ref, sxp.at[zz], rxp.at[zz], (sib, c)).wait_send()
        remote(ref, ref, sxm.at[zz], rxm.at[zz], (sib, c)).wait_send()
        remote(g_ref.at[0, lo], g_ref.at[0, lo], sop.at[zz], rop.at[zz], (sib, c)).wait_send()
        remote(g_ref.at[0, hi], g_ref.at[0, hi], som.at[zz], rom.at[zz], (sib, c)).wait_send()
    for copy in first:
        copy.wait_send()
    for k, copy in enumerate(lead_copies):
        if k == 0:
            pl.when(half != core)(copy.wait_send)
        else:
            copy.wait_send()
    for load in loads[2:]:
        load.wait()


def apply_kernel(
    starts, flags, q, z, s, t, g, q_out, z_out, s_out, t_out, q_new, z_new, band, q_sem, z_sem, b_sem
):
    r = lax.axis_index("row")
    c = lax.axis_index("col")
    word = slot_words(starts, c)
    count = jnp.int32(0)
    windows = jnp.int32(0)
    for k in range(K):
        mine = (starts[k] >> 13) == c
        count = count + jnp.where(mine, 1, 0)
        bit = jnp.left_shift(jnp.int32(1), (starts[k] >> 8) & (TILES - 1))
        windows = jnp.where(jnp.logical_and(mine, flags[k] == 1), windows | bit, windows)

    def q_copy(src, tile):
        return pltpu.make_async_copy(src, q_out.at[:, pl.ds(pl.multiple_of(tile * W, W), W)], q_sem.at[tile])

    def z_copy(src, tile):
        return pltpu.make_async_copy(src, z_out.at[:, pl.ds(pl.multiple_of(tile * W, W), W)], z_sem.at[tile])

    for tile in range(TILES):

        @pl.when(((windows >> tile) & 1) == 0)
        def _():
            q_copy(q.at[:, pl.ds(tile * W, W)], tile).start()
            z_copy(z.at[:, pl.ds(tile * W, W)], tile).start()

    def factor(side, slot):
        parts = [g[:, side, 2 * slot + h].reshape(W, W // 2) for h in range(2)]
        return jnp.concatenate(parts, axis=1)

    band_slot = jnp.int32(0)
    for j in range(SLOTS):
        k = (word >> (4 * j)) & 15
        tile = (starts[k] >> 8) & (TILES - 1)
        live = jnp.logical_and(j < count, flags[k] == 1)
        band_slot = jnp.where(jnp.logical_and(j < count, tile == r), j, band_slot)

        @pl.when(live)
        def _():
            where = pl.ds(pl.multiple_of(tile * W, W), W)
            q_new[j] = jnp.dot(q[:, where], factor(0, j), preferred_element_type=F32).astype(BF)
            q_copy(q_new.at[j], tile).start()
            z_new[j] = jnp.dot(z[:, where], factor(1, j), preferred_element_type=F32).astype(BF)
            z_copy(z_new.at[j], tile).start()

    band_live = ((windows >> r) & 1) == 1
    right = factor(1, band_slot)
    lead = jnp.concatenate([g[:, h, 2 * SLOTS].reshape(W, W // 2) for h in range(2)], axis=1)
    outs = []
    for i, (ref, out) in enumerate(((s, s_out), (t, t_out))):
        fresh = jnp.dot(ref[...], right, preferred_element_type=F32).astype(BF)
        mid = jnp.where(band_live, fresh, ref[...])
        band[i] = lax.dot_general(
            lead, mid, (((0,), (0,)), ((), ())), preferred_element_type=F32
        ).astype(BF)
        copy = pltpu.make_async_copy(band.at[i], out, b_sem.at[i])
        copy.start()
        outs.append(copy)
    for copy in outs:
        copy.wait()
    for tile in range(TILES):
        q_copy(q.at[:, pl.ds(tile * W, W)], tile).wait()
        z_copy(z.at[:, pl.ds(tile * W, W)], tile).wait()


def local(s_band, t_band, q_rows, z_rows, factors, starts, flags):
    anywhere = pl.BlockSpec(memory_space=pl.ANY)
    vmem = pl.BlockSpec(memory_space=pltpu.VMEM)
    smem = pl.BlockSpec(memory_space=pltpu.SMEM)
    dma = pltpu.SemaphoreType.DMA
    gathered, qv, zv, sv, tv = pl.pallas_call(
        gather_kernel,
        out_shape=(
            pltpu.VMEM((ROWS, UNITS, 16, 128), BF),
            pltpu.VMEM(q_rows.shape, BF),
            pltpu.VMEM(z_rows.shape, BF),
            pltpu.VMEM(s_band.shape, BF),
            pltpu.VMEM(t_band.shape, BF),
        ),
        in_specs=[anywhere] * 6,
        out_specs=[vmem] * 5,
        scratch_shapes=[
            pltpu.SMEM((K,), jnp.int32),
            pltpu.VMEM((K, 2, 8, 32), BF),
            pltpu.VMEM((K, 16, 128), F32),
            pltpu.VMEM((16, 16, 128), BF),
            pltpu.VMEM((16, 16, 128), BF),
            pltpu.VMEM((16, 128), BF),
            pltpu.VMEM((8, 16, 128), BF),
            dma((6,)),
            dma((16,)), dma((16,)), dma((8,)), dma((8,)),
            dma((8,)), dma((4,)),
            dma((4,)), dma((4,)), dma((4,)), dma((4,)),
            dma((4,)), dma((4,)), dma((4,)), dma((4,)),
            dma((20,)), dma((20,)),
        ],
        compiler_params=pltpu.CompilerParams(
            collective_id=0, has_side_effects=True, vmem_limit_bytes=32 << 20
        ),
    )(starts, factors, q_rows, z_rows, s_band, t_band)
    gathered = gathered.reshape(16, 2, UNITS, 16, 128)
    pin = lambda a: pltpu.with_memory_space_constraint(a, pltpu.VMEM)
    return tuple(
        pl.pallas_call(
            apply_kernel,
            out_shape=(
                jax.ShapeDtypeStruct(q_rows.shape, BF),
                jax.ShapeDtypeStruct(z_rows.shape, BF),
                jax.ShapeDtypeStruct(s_band.shape, BF),
                jax.ShapeDtypeStruct(t_band.shape, BF),
            ),
            in_specs=[smem, smem] + [vmem] * 5,
            out_specs=[anywhere] * 4,
            scratch_shapes=[
                pltpu.VMEM((SLOTS, 128, W), BF),
                pltpu.VMEM((SLOTS, 128, W), BF),
                pltpu.VMEM((2, W, W), BF),
                dma((TILES,)),
                dma((TILES,)),
                dma((2,)),
            ],
            compiler_params=pltpu.CompilerParams(vmem_limit_bytes=32 << 20),
        )(starts, flags, *(pin(a) for a in (qv, zv, sv, tv, gathered)))
    )


def solution(mesh):
    in_specs = (
        P(None, ("col", "row")),
        P(None, ("col", "row")),
        P("row", "col"),
        P("row", "col"),
        P(None, None, "row", "col"),
        P(),
        P(),
    )
    out_specs = (P("row", "col"), P("row", "col"), P(None, ("col", "row")), P(None, ("col", "row")))
    return jax.shard_map(local, mesh=mesh, in_specs=in_specs, out_specs=out_specs, check_vma=False)
```

time: 433 us -> 51.9 us (0.12)
  the two profiles are of different devices: /device:TPU:218 before, /device:TPU:1 now
where the time goes in v1:
time: 51.9 us; the launch traced here: 51.6 us
  Pallas kernels  44.5 us (86%)
  local copies, waits for them, and re-layouts  6.48 us (12%)
  between operations  0.66 us (1%)
    pallas_call x1, Pallas kernels, local(): pl.pallas_call(gather_kernel, out_shape=(pltpu.VMEM((ROWS, UNITS, 16, 128...  40.9 us
    unnamed x14, local copies, waits for them, and re-layouts  6.48 us
    pallas_call x1, Pallas kernels, local(): pl.pallas_call(apply_kernel, out_shape=(jax.ShapeDtypeStruct(q_rows.shape...  3.57 us

profile of v1, /device:TPU:1, one launch (start us, length us, event | category | flops | bytes accessed | tf_op | source)
XLA Modules:
  0.0 51.6 jit_solution(16202483854675282094)
XLA Ops:
  0.6 0.0 copy-start
  0.6 1.6 %copy-done = bf16[128,8192]{1,0:T(8,128)(2,1)S(1)} copy-done((bf16[128,8192]{1,0:T(8,128)(2,1)S(1)}, bf16[128,8192]{1,0:T(8,128)(2,1)}, u32[]{:S(2)}) %copy-start) | copy-done | bytes 2097176
  2.2 0.0 copy-start.1
  2.2 1.6 %copy-done.1 = bf16[128,8192]{1,0:T(8,128)(2,1)S(1)} copy-done((bf16[128,8192]{1,0:T(8,128)(2,1)S(1)}, bf16[128,8192]{1,0:T(8,128)(2,1)}, u32[]{:S(2)}) %copy-start.1) | copy-done | bytes 2097176
  3.8 0.0 copy-start.2
  3.8 0.9 %copy-done.2 = bf16[256,256]{1,0:T(8,128)(2,1)S(1)} copy-done((bf16[256,256]{1,0:T(8,128)(2,1)S(1)}, bf16[256,256]{1,0:T(8,128)(2,1)}, u32[]{:S(2)}) %copy-start.2) | copy-done | bytes 131096
  4.7 0.0 copy-start.3
  4.7 0.9 %copy-done.3 = bf16[256,256]{1,0:T(8,128)(2,1)S(1)} copy-done((bf16[256,256]{1,0:T(8,128)(2,1)S(1)}, bf16[256,256]{1,0:T(8,128)(2,1)}, u32[]{:S(2)}) %copy-start.3) | copy-done | bytes 131096
  5.6 0.0 copy-start.4
  5.6 0.8 %copy-done.4 = bf16[16,2,8,32]{3,2,1,0:T(8,128)(2,1)S(1)} copy-done((bf16[16,2,8,32]{3,2,1,0:T(8,128)(2,1)S(1)}, bf16[16,2,8,32]{3,2,1,0:T(8,128)(2,1)}, u32[]{:S(2)}) %copy-start.4) | copy-done | bytes 16408
  6.5 0.0 copy-start.5
  6.5 0.7 %copy-done.5 = s32[16]{0:T(128)S(1)} copy-done((s32[16]{0:T(128)S(1)}, s32[16]{0:T(128)}, u32[]{:S(2)}) %copy-start.5) | copy-done | bytes 88
  7.1 0.0 copy-start.6
  7.1 40.9 %shard_map.102 = (bf16[32,17,16,128]{3,2,1,0:T(8,128)(2,1)S(1)}, bf16[128,8192]{1,0:T(8,128)(2,1)S(1)}, bf16[128,8192]{1,0:T(8,128)(2,1)S(1)}, bf16[256,256]{1,0:T(8,128)(2,1)S(1)}, bf16[256,256]{1,0:T(8,128)(2,1)S(1)}) custom-call(s32[16]{0:T(128)S(1)} %copy-done.5, bf16[16,2,8,32]{3,2,1,0:T(8,128)(2,1)S(1)} %copy-done.4, bf16[128,8192]{1,0:T(8,128)(2,1)S(1)} %copy-done, ...), custom_call_target="tpu_custom_call" | custom-call | tf_op jit(solution)/shard_map/pallas_call | solution.py:327
  48.0 0.0 copy-done.6
  48.1 3.6 %shard_map.103 = (bf16[128,8192]{1,0:T(8,128)(2,1)}, bf16[128,8192]{1,0:T(8,128)(2,1)}, bf16[256,256]{1,0:T(8,128)(2,1)}, bf16[256,256]{1,0:T(8,128)(2,1)}) custom-call(s32[16]{0:T(128)S(1)} %copy-done.5, s32[16]{0:T(128)S(1)} %copy-done.6, bf16[128,8192]{1,0:T(8,128)(2,1)S(1)} %get-tuple-element.9.q, bf16[128,8192]{1,0:T(8,128)(2,1)S(1)} %get-tuple-element.10.z, ...), custom_call_target="tpu_custom_call" | custom-call | tf_op jit(solution)/shard_map/pallas_call | solution.py:360
Async XLA Ops:
  0.6 1.6 %copy-start = (bf16[128,8192]{1,0:T(8,128)(2,1)S(1)}, bf16[128,8192]{1,0:T(8,128)(2,1)}, u32[]{:S(2)}) copy-start(bf16[128,8192]{1,0:T(8,128)(2,1)} %q_hbm.1) | copy-start | bytes 6291460
  2.2 1.6 %copy-start.1 = (bf16[128,8192]{1,0:T(8,128)(2,1)S(1)}, bf16[128,8192]{1,0:T(8,128)(2,1)}, u32[]{:S(2)}) copy-start(bf16[128,8192]{1,0:T(8,128)(2,1)} %z_hbm.1) | copy-start | bytes 6291460
  3.8 0.9 %copy-start.2 = (bf16[256,256]{1,0:T(8,128)(2,1)S(1)}, bf16[256,256]{1,0:T(8,128)(2,1)}, u32[]{:S(2)}) copy-start(bf16[256,256]{1,0:T(8,128)(2,1)} %s_hbm.1) | copy-start | bytes 393220
  4.7 0.9 %copy-start.3 = (bf16[256,256]{1,0:T(8,128)(2,1)S(1)}, bf16[256,256]{1,0:T(8,128)(2,1)}, u32[]{:S(2)}) copy-start(bf16[256,256]{1,0:T(8,128)(2,1)} %t_hbm.1) | copy-start | bytes 393220
  5.6 0.8 %copy-start.4 = (bf16[16,2,8,32]{3,2,1,0:T(8,128)(2,1)S(1)}, bf16[16,2,8,32]{3,2,1,0:T(8,128)(2,1)}, u32[]{:S(2)}) copy-start(bf16[16,2,8,32]{3,2,1,0:T(8,128)(2,1)} %factors_hbm.1) | copy-start | bytes 49156
  6.5 0.7 %copy-start.5 = (s32[16]{0:T(128)S(1)}, s32[16]{0:T(128)}, u32[]{:S(2)}) copy-start(s32[16]{0:T(128)} %starts.1) | copy-start | bytes 196
  7.1 40.9 %copy-start.6 = (s32[16]{0:T(128)S(1)}, s32[16]{0:T(128)}, u32[]{:S(2)}) copy-start(s32[16]{0:T(128)} %flags.1) | copy-start | bytes 196

commit v2 on v1

--- a/solution.py
+++ b/solution.py
@@ -12,7 +12,7 @@
 ROWS = 32
 COLS = 8
 TILES = 32
-HALF = 9
+SPLIT = 12
 BF = jnp.bfloat16
 F32 = jnp.float32
 
@@ -40,7 +40,7 @@
     starts_hbm, factors_hbm, q_hbm, z_hbm, s_hbm, t_hbm,
     g_ref, qv, zv, sv, tv,
     starts_ref, fac, wide, send1, recv1, send0, recv0,
-    load_sem, ss1, rs1, ss0, rs0, sz, rz, sxp, rxp, sxm, rxm, sop, rop, som, rom, ssib, rsib,
+    load_sem, ss1, rs1, ss0, rs0, sza, rza, sxa, rxa, sxb, rxb, szb, rzb, ssib, rsib,
 ):
     r = lax.axis_index("row")
     c = lax.axis_index("col")
@@ -48,8 +48,6 @@
     x = r // 8
     zl = (r // 2) % 4
     me = core * 8 + c
-    xp = (r + 8) % ROWS
-    xm = (r + ROWS - 8) % ROWS
     sib = r + 1 - 2 * core
     base = r - core
 
@@ -69,16 +67,9 @@
     for k in range(1, 16):
         other = (me + k) % 16
         greet((base + other // 8, other % 8))
-    greet((xp, c))
-    greet((xm, c))
-
-    @pl.when(zl < 3)
-    def _():
-        greet((r + 2, c))
-
-    @pl.when(zl > 0)
-    def _():
-        greet((r - 2, c))
+    for k in range(1, 4):
+        greet(((r + 8 * k) % ROWS, c))
+        greet((x * 8 + (zl + k) % 4 * 2 + core, c))
 
     wide[...] = jnp.zeros_like(wide)
     loads[0].wait()
@@ -113,9 +104,7 @@
         [jnp.where(core == 0, placed, nothing), jnp.where(core == 1, placed, nothing)], axis=0
     ).astype(BF)
 
-    pl.semaphore_wait(
-        barrier, 17 + jnp.where(zl < 3, 1, 0) + jnp.where(zl > 0, 1, 0)
-    )
+    pl.semaphore_wait(barrier, 21)
 
     first = []
     for k in range(1, 16):
@@ -177,71 +166,67 @@
         jnp.where(zl < 2, 2, jnp.where(zl == 2, 3, 1)),
         jnp.where(zl < 2, 3, 0),
     ]
-
-    def block(xx, zz):
-        return ((xx + 4) % 4) * 8 + zz * 2 + core
-
-    def to_sibling(ref, n):
-        remote(ref, ref, ssib.at[n], rsib.at[n], (sib, c)).start()
-
-    lo = pl.ds(0, HALF)
-    hi = pl.ds(HALF, UNITS - HALF)
-
-    def opposite(i, start):
+    lo = pl.ds(0, SPLIT)
+    hi = pl.ds(SPLIT, UNITS - SPLIT)
+    ends = []
+
+    def send(ref, send_sem, recv_sem, device):
+        copy = remote(ref, ref, send_sem, recv_sem, device)
+        copy.start()
+        ends.append(copy)
+
+    def got(ref, recv_sem):
+        remote(ref, ref, load_sem.at[0], recv_sem, (sib, c)).wait_recv()
+
+    def at(xx, zz, which):
+        return g_ref.at[xx * 8 + zz * 2 + core, which]
+
+    xs = [(x + k) % 4 for k in range(4)]
+    zs = [(zl + k) % 4 for k in range(4)]
+
+    def along_x(zz, i, which, send_sems, recv_sem):
+        for k in (1, 3, 2):
+            send(at(x, zz, which), send_sems.at[4 * i + k], recv_sem, (xs[k] * 8 + r % 8, c))
+
+    def along_z(xx, i, which, send_sems, recv_sem):
+        for k in (1, 3, 2):
+            send(at(xx, zl, which), send_sems.at[4 * i + k], recv_sem, (x * 8 + zs[k] * 2 + core, c))
+
+    def across(xx, zz, which, n):
+        spot = 16 * n + xx * 4 + zz
+        send(at(xx, zz, which), ssib.at[spot], rsib.at[spot], (sib, c))
+
+    along_z(x, 0, lo, sza, rza.at[zl])
+    along_x(zl, 0, hi, sxb, rxb.at[x])
+    along_x(zl, 0, lo, sxa, rxa.at[x * 4 + zl])
+    along_z(x, 0, hi, szb, rzb.at[x * 4 + zl])
+    across(x, zl, lo, 0)
+    across(x, zl, hi, 1)
+    for i in (1, 2, 3):
+        xx = xs[(0, 1, 3, 2)[i]]
+        got(at(xx, zl, hi), rxb.at[xx])
+        along_z(xx, i, hi, szb, rzb.at[xx * 4 + zl])
         zz = order[i]
-        b = block(x + 2, zz)
-        remote(g_ref.at[b, lo], g_ref.at[b, lo], sop.at[zz], rop.at[zz], (sib, c)).wait_recv()
-        to_sibling(g_ref.at[b, lo], 12 + zz)
-        remote(g_ref.at[b, hi], g_ref.at[b, hi], som.at[zz], rom.at[zz], (sib, c)).wait_recv()
-        to_sibling(g_ref.at[b, hi], 16 + zz)
-
-    ups, downs = [], []
+        got(at(x, zz, lo), rza.at[zz])
+        along_x(zz, i, lo, sxa, rxa.at[x * 4 + zz])
+        across(xx, zl, hi, 1)
+        across(x, zz, lo, 0)
     for i in range(4):
-        zz = order[i]
-        own = g_ref.at[block(x, zz)]
-        if i:
-            remote(own, own, sz.at[0], rz.at[zz], (sib, c)).wait_recv()
-        up = remote(own, own, sz.at[zz], rz.at[zz], (r + 2, c))
-        down = remote(own, own, sz.at[4 + zz], rz.at[zz], (r - 2, c))
-        goes_up = jnp.logical_and(zz <= zl, zl < 3)
-        goes_down = jnp.logical_and(zz >= zl, zl > 0)
-        pl.when(goes_up)(up.start)
-        pl.when(goes_down)(down.start)
-        ups.append((goes_up, up))
-        downs.append((goes_down, down))
-        remote(own, own, sxp.at[zz], rxp.at[zz], (xp, c)).start()
-        remote(own, own, sxm.at[zz], rxm.at[zz], (xm, c)).start()
-        to_sibling(own, zz)
-        b = block(x - 1, zz)
-        remote(g_ref.at[b], g_ref.at[b], sxp.at[zz], rxp.at[zz], (sib, c)).wait_recv()
-        remote(g_ref.at[b, lo], g_ref.at[b, lo], sop.at[zz], rop.at[zz], (xp, c)).start()
-        to_sibling(g_ref.at[b], 4 + zz)
-        b = block(x + 1, zz)
-        remote(g_ref.at[b], g_ref.at[b], sxm.at[zz], rxm.at[zz], (sib, c)).wait_recv()
-        remote(g_ref.at[b, hi], g_ref.at[b, hi], som.at[zz], rom.at[zz], (xm, c)).start()
-        to_sibling(g_ref.at[b], 8 + zz)
-        if i:
-            opposite(i - 1, False)
-    opposite(3, False)
-
-    theirs = 1 - core
-    for n in range(20):
-        if n < 12:
-            b = ((x + (0, 3, 1)[n // 4]) % 4) * 8 + (n % 4) * 2 + theirs
-            ref = g_ref.at[b]
-        else:
-            b = ((x + 2) % 4) * 8 + (n % 4) * 2 + theirs
-            ref = g_ref.at[b, lo if n < 16 else hi]
-        remote(ref, ref, ssib.at[n], rsib.at[n], (sib, c)).wait_recv()
-        remote(ref, ref, ssib.at[n], rsib.at[n], (sib, c)).wait_send()
-    for goes, copy in ups + downs:
-        pl.when(goes)(copy.wait_send)
-    for zz in range(4):
-        ref = g_ref.at[0]
-        remote(ref, ref, sxp.at[zz], rxp.at[zz], (sib, c)).wait_send()
-        remote(ref, ref, sxm.at[zz], rxm.at[zz], (sib, c)).wait_send()
-        remote(g_ref.at[0, lo], g_ref.at[0, lo], sop.at[zz], rop.at[zz], (sib, c)).wait_send()
-        remote(g_ref.at[0, hi], g_ref.at[0, hi], som.at[zz], rom.at[zz], (sib, c)).wait_send()
+        for k in (1, 3, 2):
+            zz = order[i]
+            got(at(xs[k], zz, lo), rxa.at[xs[k] * 4 + zz])
+            across(xs[k], zz, lo, 0)
+            xx = xs[(0, 1, 3, 2)[i]]
+            zz = order[(0, 1, 2, 3)[(0, 1, 3, 2)[k]]]
+            got(at(xx, zz, hi), rzb.at[xx * 4 + zz])
+            across(xx, zz, hi, 1)
+
+    for spot in range(16):
+        b = 2 * spot + 1 - core
+        got(g_ref.at[b, lo], rsib.at[spot])
+        got(g_ref.at[b, hi], rsib.at[16 + spot])
+    for copy in ends:
+        copy.wait_send()
     for copy in first:
         copy.wait_send()
     for k, copy in enumerate(lead_copies):
@@ -321,6 +306,7 @@
 
 def local(s_band, t_band, q_rows, z_rows, factors, starts, flags):
     anywhere = pl.BlockSpec(memory_space=pl.ANY)
+    hbm = pl.BlockSpec(memory_space=pltpu.HBM)
     vmem = pl.BlockSpec(memory_space=pltpu.VMEM)
     smem = pl.BlockSpec(memory_space=pltpu.SMEM)
     dma = pltpu.SemaphoreType.DMA
@@ -333,7 +319,7 @@
             pltpu.VMEM(s_band.shape, BF),
             pltpu.VMEM(t_band.shape, BF),
         ),
-        in_specs=[anywhere] * 6,
+        in_specs=[hbm] * 6,
         out_specs=[vmem] * 5,
         scratch_shapes=[
             pltpu.SMEM((K,), jnp.int32),
@@ -345,15 +331,14 @@
             pltpu.VMEM((8, 16, 128), BF),
             dma((6,)),
             dma((16,)), dma((16,)), dma((8,)), dma((8,)),
-            dma((8,)), dma((4,)),
-            dma((4,)), dma((4,)), dma((4,)), dma((4,)),
-            dma((4,)), dma((4,)), dma((4,)), dma((4,)),
-            dma((20,)), dma((20,)),
+            dma((4,)), dma((4,)), dma((16,)), dma((16,)),
+            dma((4,)), dma((4,)), dma((16,)), dma((16,)),
+            dma((32,)), dma((32,)),
         ],
         compiler_params=pltpu.CompilerParams(
             collective_id=0, has_side_effects=True, vmem_limit_bytes=32 << 20
         ),
-    )(starts, factors, q_rows, z_rows, s_band, t_band)
+    )(*(pltpu.with_memory_space_constraint(a, pltpu.HBM) for a in (starts, factors, q_rows, z_rows, s_band, t_band)))
     gathered = gathered.reshape(16, 2, UNITS, 16, 128)
     pin = lambda a: pltpu.with_memory_space_constraint(a, pltpu.VMEM)
     return tuple(

time: 51.9 us -> 37.8 us (0.73)
  Pallas kernels: 44.5 us -> 37 us
  local copies, waits for them, and re-layouts: 6.48 us -> 0.01 us
    pallas_call x1, Pallas kernels: 40.9 us -> 33.6 us  [local(): pl.pallas_call(gather_kernel, out_shape=(pltpu.VMEM((ROWS, UNITS, 16, 128...]
    unnamed x14 -> x4, local copies, waits for them, and re-layouts: 6.48 us -> 0.01 us
where the time goes in v2:
time: 37.8 us; the launch traced here: 37.7 us
  Pallas kernels  37 us (98%)
  between operations  0.67 us (2%)
    pallas_call x1, Pallas kernels, local(): pl.pallas_call(gather_kernel, out_shape=(pltpu.VMEM((ROWS, UNITS, 16, 128...  33.6 us
    pallas_call x1, Pallas kernels, local(): pl.pallas_call(apply_kernel, out_shape=(jax.ShapeDtypeStruct(q_rows.shape...  3.38 us

profile of v2, /device:TPU:1, one launch (start us, length us, event | category | flops | bytes accessed | tf_op | source)
XLA Modules:
  0.0 37.7 jit_solution(11116159962745716954)
XLA Ops:
  0.6 0.0 copy-start
  0.6 0.0 copy-start.1
  0.7 33.6 %shard_map.102 = (bf16[32,17,16,128]{3,2,1,0:T(8,128)(2,1)S(1)}, bf16[128,8192]{1,0:T(8,128)(2,1)S(1)}, bf16[128,8192]{1,0:T(8,128)(2,1)S(1)}, bf16[256,256]{1,0:T(8,128)(2,1)S(1)}, bf16[256,256]{1,0:T(8,128)(2,1)S(1)}) custom-call(s32[16]{0:T(128)} %starts.1, bf16[16,2,8,32]{3,2,1,0:T(8,128)(2,1)} %factors_hbm.1, bf16[128,8192]{1,0:T(8,128)(2,1)} %q_hbm.1, ...), custom_call_target="tpu_custom_call" | custom-call | tf_op jit(solution)/shard_map/pallas_call | solution.py:313
  34.3 0.0 copy-done
  34.3 0.0 copy-done.1
  34.3 3.4 %shard_map.103 = (bf16[128,8192]{1,0:T(8,128)(2,1)}, bf16[128,8192]{1,0:T(8,128)(2,1)}, bf16[256,256]{1,0:T(8,128)(2,1)}, bf16[256,256]{1,0:T(8,128)(2,1)}) custom-call(s32[16]{0:T(128)S(1)} %copy-done, s32[16]{0:T(128)S(1)} %copy-done.1, bf16[128,8192]{1,0:T(8,128)(2,1)S(1)} %get-tuple-element.9.q, bf16[128,8192]{1,0:T(8,128)(2,1)S(1)} %get-tuple-element.10.z, ...), custom_call_target="tpu_custom_call" | custom-call | tf_op jit(solution)/shard_map/pallas_call | solution.py:345
Async XLA Ops:
  0.6 33.6 %copy-start = (s32[16]{0:T(128)S(1)}, s32[16]{0:T(128)}, u32[]{:S(2)}) copy-start(s32[16]{0:T(128)} %starts.1) | copy-start | bytes 196
  0.6 33.6 %copy-start.1 = (s32[16]{0:T(128)S(1)}, s32[16]{0:T(128)}, u32[]{:S(2)}) copy-start(s32[16]{0:T(128)} %flags.1) | copy-start | bytes 196

commit v3 on v2

v3 whole, which is shorter than its diff:
```python
import jax
import jax.numpy as jnp
from jax import lax
from jax.experimental import pallas as pl
from jax.experimental.pallas import tpu as pltpu
from jax.sharding import PartitionSpec as P

W = 256
K = 16
SLOTS = 8
UNITS = SLOTS + 1
ROWS = 32
COLS = 8
TILES = 32
SPLIT = 7
BF = jnp.bfloat16
F32 = jnp.float32


def slot_words(starts_ref, column):
    word = jnp.int32(0)
    for k in reversed(range(K)):
        mine = (starts_ref[k] >> 13) == column
        word = jnp.where(mine, (word << 4) | k, word)
    return word


def remote(src, dst, send_sem, recv_sem, device):
    return pltpu.make_async_remote_copy(
        src_ref=src,
        dst_ref=dst,
        send_sem=send_sem,
        recv_sem=recv_sem,
        device_id=device,
        device_id_type=pl.DeviceIdType.MESH,
    )


def gather_kernel(
    starts_hbm, factors_hbm, q_hbm, z_hbm, s_hbm, t_hbm,
    g_ref, qv, zv, sv, tv,
    starts_ref, fac, wide, send1, recv1, send0, recv0,
    load_sem, ss1, rs1, ss0, rs0, sza, rza, sxa, rxa, sxb, rxb, szb, rzb, ssib, rsib,
):
    r = lax.axis_index("row")
    c = lax.axis_index("col")
    core = r % 2
    x = r // 8
    zl = (r // 2) % 4
    far_half = c // 4
    y = c % 4
    me = core * 4 + y
    sib = r + 1 - 2 * core
    near_base = r - core
    far_base = x * 8 + (3 - zl) * 2
    near_col = far_half * 4
    far_col = (1 - far_half) * 4

    barrier = pltpu.get_barrier_semaphore()

    def greet(device):
        pl.semaphore_signal(barrier, inc=1, device_id=device, device_id_type=pl.DeviceIdType.MESH)

    loads = [
        pltpu.make_async_copy(a, b, load_sem.at[i])
        for i, (a, b) in enumerate(
            [(factors_hbm, fac), (starts_hbm, starts_ref), (q_hbm, qv), (z_hbm, zv), (s_hbm, sv), (t_hbm, tv)]
        )
    ]
    loads[0].start()
    loads[1].start()

    @pl.when(far_half == 0)
    def _():
        for k in range(8):
            greet((far_base + k // 4, far_col + k % 4))

    for k in range(1, 8):
        other = (me + k) % 8
        greet((near_base + other // 4, near_col + other % 4))
    for k in range(1, 4):
        greet(((r + 8 * k) % ROWS, c))
        greet((x * 8 + (zl + k) % 4 * 2 + core, c))

    wide[...] = jnp.zeros_like(wide)
    loads[0].wait()
    loads[1].wait()
    for load in loads[2:]:
        load.start()
    for k in range(K):
        for m in range(2):
            wide[k, 8 * m : 8 * m + 8, 0:32] = fac[k, m].astype(F32)
    for wave in (1, 0):
        for dest in range(4):
            word = slot_words(starts_ref, (far_col if wave else near_col) + dest)
            rows = []
            for a in range(2):
                total = None
                for b in range(4):
                    k = (word >> (4 * (4 * a + b))) & 15
                    piece = wide[k]
                    if b:
                        piece = pltpu.roll(piece, 32 * b, 1)
                    total = piece if total is None else total + piece
                rows.append(total)
            for m in range(2):
                send1[wave, m * 4 + dest] = jnp.concatenate(
                    [rows[0][8 * m : 8 * m + 8], rows[1][8 * m : 8 * m + 8]], axis=0
                ).astype(BF)
    lead = wide[0, 0:8]
    placed = lead
    for b in range(1, 4):
        placed = jnp.where(y == b, pltpu.roll(lead, 32 * b, 1), placed)
    nothing = jnp.zeros_like(placed)
    send0[...] = jnp.concatenate(
        [jnp.where(core == 0, placed, nothing), jnp.where(core == 1, placed, nothing)], axis=0
    ).astype(BF)

    def far_piece(k):
        device = (far_base + k // 4, far_col + k % 4)
        return remote(send1.at[1, k], recv1.at[1, me], ss1.at[8 + k], rs1.at[8 + me], device)

    def far_lead(k):
        return remote(send0, recv0.at[me], ss0.at[4 + k], rs0.at[me], (far_base + 1, far_col + k))

    def near_piece(k):
        other = (me + k) % 8
        device = (near_base + other // 4, near_col + other % 4)
        return remote(send1.at[0, other], recv1.at[0, me], ss1.at[k], rs1.at[me], device)

    def near_lead(k):
        return remote(send0, recv0.at[me], ss0.at[k], rs0.at[me], (near_base, near_col + (y + k) % 4))

    def got(ref, recv_sem):
        remote(ref, ref, load_sem.at[0], recv_sem, (sib, c)).wait_recv()

    @pl.when(far_half == 1)
    def _():
        pl.semaphore_wait(barrier, 21)
        for k in range(8):
            far_piece(k).start()
        for k in range(4):
            far_lead(k).start()

    @pl.when(far_half == 0)
    def _():
        pl.semaphore_wait(barrier, 13)

    for k in range(1, 8):
        near_piece(k).start()
    pl.when(core == 1)(near_lead(0).start)
    for k in range(1, 4):
        near_lead(k).start()
    recv1[0, me] = send1[0, me]

    @pl.when(core == 0)
    def _():
        recv0[me] = send0[...]

    lane = lax.broadcasted_iota(jnp.int32, (16, 128), 1) // 32

    def unpack(wave):
        spot = far_base + core if wave else r
        turned = {}
        for s in range(2):
            for cc in range(4):
                piece = recv1[wave, s * 4 + cc].astype(F32)
                for turn in range(4):
                    turned[s, cc, turn] = pltpu.roll(piece, 32 * turn, 1) if turn else piece
        for b in range(4):
            joined = []
            for s in range(2):
                out = turned[s, 0, (0 - b) % 4]
                for cc in range(1, 4):
                    out = jnp.where(lane == cc, turned[s, cc, (cc - b) % 4], out)
                joined.append(out)
            for a in range(2):
                g_ref[wave, spot, 4 * a + b] = jnp.concatenate(
                    [joined[0][8 * a : 8 * a + 8], joined[1][8 * a : 8 * a + 8]], axis=0
                ).astype(BF)

        @pl.when(core == wave)
        def _():
            total = recv0[0].astype(F32)
            for k in range(1, 8):
                total = total + recv0[k].astype(F32)
            g_ref[wave, spot, SLOTS] = total.astype(BF)

        @pl.when(core != wave)
        def _():
            g_ref[wave, spot, SLOTS] = jnp.zeros((16, 128), BF)

    order = [
        zl,
        jnp.where(zl == 0, 1, jnp.where(zl == 1, 0, jnp.where(zl == 2, 1, 2))),
        jnp.where(zl < 2, 2, jnp.where(zl == 2, 3, 1)),
        jnp.where(zl < 2, 3, 0),
    ]
    lo = pl.ds(0, SPLIT)
    hi = pl.ds(SPLIT, UNITS - SPLIT)
    xs = [(x + k) % 4 for k in range(4)]
    zs = [(zl + k) % 4 for k in range(4)]
    nearest = (0, 1, 3, 2)

    def at(wave, xx, zz, which):
        return g_ref.at[wave, xx * 8 + (3 - zz if wave else zz) * 2 + core, which]

    def send(ref, send_sem, recv_sem, device):
        remote(ref, ref, send_sem, recv_sem, device).start()

    def along_x(wave, zz, i, which, send_sems, recv_sem):
        for k in (1, 3, 2):
            send(at(wave, x, zz, which), send_sems.at[wave, 4 * i + k], recv_sem, (xs[k] * 8 + r % 8, c))

    def along_z(wave, xx, i, which, send_sems, recv_sem):
        for k in (1, 3, 2):
            device = (x * 8 + zs[k] * 2 + core, c)
            send(at(wave, xx, zl, which), send_sems.at[wave, 4 * i + k], recv_sem, device)

    def across(wave, xx, zz, which, n):
        spot = 16 * n + xx * 4 + zz
        send(at(wave, xx, zz, which), ssib.at[wave, spot], rsib.at[wave, spot], (sib, c))

    def first_leg(wave):
        along_z(wave, x, 0, lo, sza, rza.at[wave, zl])
        along_x(wave, zl, 0, hi, sxb, rxb.at[wave, x])
        along_x(wave, zl, 0, lo, sxa, rxa.at[wave, x * 4 + zl])
        along_z(wave, x, 0, hi, szb, rzb.at[wave, x * 4 + zl])
        across(wave, x, zl, lo, 0)
        across(wave, x, zl, hi, 1)

    def second_leg(wave):
        for i in (1, 2, 3):
            xx = xs[nearest[i]]
            got(at(wave, xx, zl, hi), rxb.at[wave, xx])
            along_z(wave, xx, i, hi, szb, rzb.at[wave, xx * 4 + zl])
            zz = order[i]
            got(at(wave, x, zz, lo), rza.at[wave, zz])
            along_x(wave, zz, i, lo, sxa, rxa.at[wave, x * 4 + zz])
            across(wave, xx, zl, hi, 1)
            across(wave, x, zz, lo, 0)

    def last_leg(wave):
        for i in range(4):
            for k in (1, 2, 3):
                zz, xx = order[i], xs[nearest[k]]
                got(at(wave, xx, zz, lo), rxa.at[wave, xx * 4 + zz])
                across(wave, xx, zz, lo, 0)
                zz, xx = order[k], xs[nearest[i]]
                got(at(wave, xx, zz, hi), rzb.at[wave, xx * 4 + zz])
                across(wave, xx, zz, hi, 1)

    for k in range(1, 8):
        other = (me + k) % 8
        got(recv1.at[0, other], rs1.at[other])

    @pl.when(core == 0)
    def _():
        for k in range(1, 8):
            other = (me + k) % 8
            got(recv0.at[other], rs0.at[other])

    unpack(0)
    first_leg(0)

    @pl.when(far_half == 1)
    def _():
        second_leg(0)

    for k in range(8):
        got(recv1.at[1, k], rs1.at[8 + k])

        @pl.when(far_half == 0)
        def _():
            far_piece(k).start()
            if k >= 4:
                far_lead(k - 4).start()

    @pl.when(core == 1)
    def _():
        for k in range(8):
            got(recv0.at[k], rs0.at[k])

    unpack(1)
    first_leg(1)

    @pl.when(far_half == 0)
    def _():
        second_leg(0)

    second_leg(1)
    last_leg(0)
    last_leg(1)

    for wave in range(2):
        for spot in range(16):
            zz = spot % 4
            b = (spot // 4) * 8 + (3 - zz if wave else zz) * 2 + 1 - core
            got(g_ref.at[wave, b, lo], rsib.at[wave, spot])
            got(g_ref.at[wave, b, hi], rsib.at[wave, 16 + spot])

    def left(ref, send_sem):
        remote(ref, ref, send_sem, load_sem.at[0], (sib, c)).wait_send()

    for wave in range(2):
        small, large = g_ref.at[wave, 0, hi], g_ref.at[wave, 0, lo]
        for k in (1, 2, 3):
            left(large, sza.at[wave, k])
            left(small, sxb.at[wave, k])
            for i in range(4):
                left(large, sxa.at[wave, 4 * i + k])
                left(small, szb.at[wave, 4 * i + k])
        for spot in range(16):
            left(large, ssib.at[wave, spot])
            left(small, ssib.at[wave, 16 + spot])
    for k in range(8):
        left(send1.at[1, k], ss1.at[8 + k])
        if k:
            left(send1.at[0, k], ss1.at[k])
    for k in range(8):
        if k:
            left(send0, ss0.at[k])
        else:
            pl.when(core == 1)(near_lead(0).wait_send)
    for load in loads[2:]:
        load.wait()


def apply_kernel(
    starts, flags, q, z, s, t, g, q_out, z_out, s_out, t_out, q_new, z_new, band, q_sem, z_sem, b_sem, whole_sem
):
    r = lax.axis_index("row")
    c = lax.axis_index("col")
    word = slot_words(starts, c)
    count = jnp.int32(0)
    windows = jnp.int32(0)
    for k in range(K):
        mine = (starts[k] >> 13) == c
        count = count + jnp.where(mine, 1, 0)
        bit = jnp.left_shift(jnp.int32(1), (starts[k] >> 8) & (TILES - 1))
        windows = jnp.where(jnp.logical_and(mine, flags[k] == 1), windows | bit, windows)

    wholes = [pltpu.make_async_copy(q, q_out, whole_sem.at[0]), pltpu.make_async_copy(z, z_out, whole_sem.at[1])]
    for whole in wholes:
        whole.start()

    def q_copy(j, tile):
        return pltpu.make_async_copy(q_new.at[j], q_out.at[:, pl.ds(pl.multiple_of(tile * W, W), W)], q_sem.at[j])

    def z_copy(j, tile):
        return pltpu.make_async_copy(z_new.at[j], z_out.at[:, pl.ds(pl.multiple_of(tile * W, W), W)], z_sem.at[j])

    far_half = c // 4

    def factor(side, slot):
        parts = [g[h ^ far_half, :, side, slot].reshape(W, W // 2) for h in range(2)]
        return jnp.concatenate(parts, axis=1)

    band_slot = jnp.int32(0)
    slots = []
    for j in range(SLOTS):
        k = (word >> (4 * j)) & 15
        tile = (starts[k] >> 8) & (TILES - 1)
        live = jnp.logical_and(j < count, flags[k] == 1)
        band_slot = jnp.where(jnp.logical_and(j < count, tile == r), j, band_slot)
        slots.append((live, tile))

        @pl.when(live)
        def _():
            where = pl.ds(pl.multiple_of(tile * W, W), W)
            q_new[j] = jnp.dot(q[:, where], factor(0, j), preferred_element_type=F32).astype(BF)
            z_new[j] = jnp.dot(z[:, where], factor(1, j), preferred_element_type=F32).astype(BF)

    band_live = ((windows >> r) & 1) == 1
    right = factor(1, band_slot)
    lead = jnp.concatenate(
        [g[h ^ far_half, :, h ^ far_half, SLOTS].reshape(W, W // 2) for h in range(2)], axis=1
    )
    outs = []
    for i, (ref, out) in enumerate(((s, s_out), (t, t_out))):
        fresh = jnp.dot(ref[...], right, preferred_element_type=F32).astype(BF)
        mid = jnp.where(band_live, fresh, ref[...])
        band[i] = lax.dot_general(
            lead, mid, (((0,), (0,)), ((), ())), preferred_element_type=F32
        ).astype(BF)
        copy = pltpu.make_async_copy(band.at[i], out, b_sem.at[i])
        copy.start()
        outs.append(copy)
    for whole in wholes:
        whole.wait()
    for j, (live, tile) in enumerate(slots):

        @pl.when(live)
        def _():
            q_copy(j, tile).start()
            z_copy(j, tile).start()

    for copy in outs:
        copy.wait()
    for j, (live, tile) in enumerate(slots):

        @pl.when(live)
        def _():
            q_copy(j, tile).wait()
            z_copy(j, tile).wait()


def local(s_band, t_band, q_rows, z_rows, factors, starts, flags):
    anywhere = pl.BlockSpec(memory_space=pl.ANY)
    hbm = pl.BlockSpec(memory_space=pltpu.HBM)
    vmem = pl.BlockSpec(memory_space=pltpu.VMEM)
    smem = pl.BlockSpec(memory_space=pltpu.SMEM)
    dma = pltpu.SemaphoreType.DMA
    gathered, qv, zv, sv, tv = pl.pallas_call(
        gather_kernel,
        out_shape=(
            pltpu.VMEM((2, ROWS, UNITS, 16, 128), BF),
            pltpu.VMEM(q_rows.shape, BF),
            pltpu.VMEM(z_rows.shape, BF),
            pltpu.VMEM(s_band.shape, BF),
            pltpu.VMEM(t_band.shape, BF),
        ),
        in_specs=[hbm] * 6,
        out_specs=[vmem] * 5,
        scratch_shapes=[
            pltpu.SMEM((K,), jnp.int32),
            pltpu.VMEM((K, 2, 8, 32), BF),
            pltpu.VMEM((K, 16, 128), F32),
            pltpu.VMEM((2, 8, 16, 128), BF),
            pltpu.VMEM((2, 8, 16, 128), BF),
            pltpu.VMEM((16, 128), BF),
            pltpu.VMEM((8, 16, 128), BF),
            dma((6,)),
            dma((16,)), dma((16,)), dma((8,)), dma((8,)),
            dma((2, 4)), dma((2, 4)), dma((2, 16)), dma((2, 16)),
            dma((2, 4)), dma((2, 4)), dma((2, 16)), dma((2, 16)),
            dma((2, 32)), dma((2, 32)),
        ],
        compiler_params=pltpu.CompilerParams(
            collective_id=0, has_side_effects=True, vmem_limit_bytes=32 << 20
        ),
    )(*(pltpu.with_memory_space_constraint(a, pltpu.HBM) for a in (starts, factors, q_rows, z_rows, s_band, t_band)))
    gathered = gathered.reshape(2, 16, 2, UNITS, 16, 128)
    pin = lambda a: pltpu.with_memory_space_constraint(a, pltpu.VMEM)
    return tuple(
        pl.pallas_call(
            apply_kernel,
            out_shape=(
                jax.ShapeDtypeStruct(q_rows.shape, BF),
                jax.ShapeDtypeStruct(z_rows.shape, BF),
                jax.ShapeDtypeStruct(s_band.shape, BF),
                jax.ShapeDtypeStruct(t_band.shape, BF),
            ),
            in_specs=[smem, smem] + [vmem] * 5,
            out_specs=[anywhere] * 4,
            scratch_shapes=[
                pltpu.VMEM((SLOTS, 128, W), BF),
                pltpu.VMEM((SLOTS, 128, W), BF),
                pltpu.VMEM((2, W, W), BF),
                dma((SLOTS,)),
                dma((SLOTS,)),
                dma((2,)),
                dma((2,)),
            ],
            compiler_params=pltpu.CompilerParams(vmem_limit_bytes=32 << 20),
        )(starts, flags, *(pin(a) for a in (qv, zv, sv, tv, gathered)))
    )


def solution(mesh):
    in_specs = (
        P(None, ("col", "row")),
        P(None, ("col", "row")),
        P("row", "col"),
        P("row", "col"),
        P(None, None, "row", "col"),
        P(),
        P(),
    )
    out_specs = (P("row", "col"), P("row", "col"), P(None, ("col", "row")), P(None, ("col", "row")))
    return jax.shard_map(local, mesh=mesh, in_specs=in_specs, out_specs=out_specs, check_vma=False)
```

time: 37.8 us -> 35.8 us (0.947)
  Pallas kernels: 37 us -> 35 us
    pallas_call x1, Pallas kernels: 33.6 us -> 31.5 us  [local(): pl.pallas_call(gather_kernel, out_shape=(pltpu.VMEM((2, ROWS, UNITS, 16,...]
where the time goes in v3:
time: 35.8 us; the launch traced here: 35.7 us
  Pallas kernels  35 us (98%)
  between operations  0.67 us (2%)
    pallas_call x1, Pallas kernels, local(): pl.pallas_call(gather_kernel, out_shape=(pltpu.VMEM((2, ROWS, UNITS, 16,...  31.5 us
    pallas_call x1, Pallas kernels, local(): pl.pallas_call(apply_kernel, out_shape=(jax.ShapeDtypeStruct(q_rows.shape...  3.47 us

profile of v3, /device:TPU:1, one launch (start us, length us, event | category | flops | bytes accessed | tf_op | source)
XLA Modules:
  0.0 35.7 jit_solution(15746991880057900125)
XLA Ops:
  0.6 0.0 copy-start
  0.6 0.0 copy-start.1
  0.7 31.5 %shard_map.102 = (bf16[2,32,9,16,128]{4,3,2,1,0:T(8,128)(2,1)S(1)}, bf16[128,8192]{1,0:T(8,128)(2,1)S(1)}, bf16[128,8192]{1,0:T(8,128)(2,1)S(1)}, bf16[256,256]{1,0:T(8,128)(2,1)S(1)}, bf16[256,256]{1,0:T(8,128)(2,1)S(1)}) custom-call(s32[16]{0:T(128)} %starts.1, bf16[16,2,8,32]{3,2,1,0:T(8,128)(2,1)} %factors_hbm.1, bf16[128,8192]{1,0:T(8,128)(2,1)} %q_hbm.1, ...), custom_call_target="tpu_custom_call" | custom-call | tf_op jit(solution)/shard_map/pallas_call | solution.py:414
  32.2 0.0 copy-done
  32.2 0.0 copy-done.1
  32.2 3.5 %shard_map.103 = (bf16[128,8192]{1,0:T(8,128)(2,1)}, bf16[128,8192]{1,0:T(8,128)(2,1)}, bf16[256,256]{1,0:T(8,128)(2,1)}, bf16[256,256]{1,0:T(8,128)(2,1)}) custom-call(s32[16]{0:T(128)S(1)} %copy-done, s32[16]{0:T(128)S(1)} %copy-done.1, bf16[128,8192]{1,0:T(8,128)(2,1)S(1)} %get-tuple-element.9.q, bf16[128,8192]{1,0:T(8,128)(2,1)S(1)} %get-tuple-element.10.z, ...), custom_call_target="tpu_custom_call" | custom-call | tf_op jit(solution)/shard_map/pallas_call | solution.py:446
Async XLA Ops:
  0.6 31.5 %copy-start = (s32[16]{0:T(128)S(1)}, s32[16]{0:T(128)}, u32[]{:S(2)}) copy-start(s32[16]{0:T(128)} %starts.1) | copy-start | bytes 196
  0.6 31.5 %copy-start.1 = (s32[16]{0:T(128)S(1)}, s32[16]{0:T(128)}, u32[]{:S(2)}) copy-start(s32[16]{0:T(128)} %flags.1) | copy-start | bytes 196

commit v4 on v3

--- a/solution.py
+++ b/solution.py
@@ -40,7 +40,7 @@
     starts_hbm, factors_hbm, q_hbm, z_hbm, s_hbm, t_hbm,
     g_ref, qv, zv, sv, tv,
     starts_ref, fac, wide, send1, recv1, send0, recv0,
-    load_sem, ss1, rs1, ss0, rs0, sza, rza, sxa, rxa, sxb, rxb, szb, rzb, ssib, rsib,
+    load_sem, sent1, sent0, came1, came0, sent, line_sem, ring_sem, group_sem, sib_sem,
 ):
     r = lax.axis_index("row")
     c = lax.axis_index("col")
@@ -118,18 +118,19 @@
 
     def far_piece(k):
         device = (far_base + k // 4, far_col + k % 4)
-        return remote(send1.at[1, k], recv1.at[1, me], ss1.at[8 + k], rs1.at[8 + me], device)
+        return remote(send1.at[1, k], recv1.at[1, me], sent1.at[1], came1.at[1], device)
 
     def far_lead(k):
-        return remote(send0, recv0.at[me], ss0.at[4 + k], rs0.at[me], (far_base + 1, far_col + k))
+        return remote(send0, recv0.at[me], sent0.at[1], came0, (far_base + 1, far_col + k))
 
     def near_piece(k):
         other = (me + k) % 8
         device = (near_base + other // 4, near_col + other % 4)
-        return remote(send1.at[0, other], recv1.at[0, me], ss1.at[k], rs1.at[me], device)
+        return remote(send1.at[0, other], recv1.at[0, me], sent1.at[0], came1.at[0], device)
 
     def near_lead(k):
-        return remote(send0, recv0.at[me], ss0.at[k], rs0.at[me], (near_base, near_col + (y + k) % 4))
+        sem = sent0.at[0] if k else sent0.at[2]
+        return remote(send0, recv0.at[me], sem, came0, (near_base, near_col + (y + k) % 4))
 
     def got(ref, recv_sem):
         remote(ref, ref, load_sem.at[0], recv_sem, (sib, c)).wait_recv()
@@ -198,6 +199,7 @@
     ]
     lo = pl.ds(0, SPLIT)
     hi = pl.ds(SPLIT, UNITS - SPLIT)
+    whole = pl.ds(0, UNITS)
     xs = [(x + k) % 4 for k in range(4)]
     zs = [(zl + k) % 4 for k in range(4)]
     nearest = (0, 1, 3, 2)
@@ -205,60 +207,50 @@
     def at(wave, xx, zz, which):
         return g_ref.at[wave, xx * 8 + (3 - zz if wave else zz) * 2 + core, which]
 
-    def send(ref, send_sem, recv_sem, device):
-        remote(ref, ref, send_sem, recv_sem, device).start()
-
-    def along_x(wave, zz, i, which, send_sems, recv_sem):
+    def send(ref, recv_sem, device, wave):
+        remote(ref, ref, sent.at[wave], recv_sem, device).start()
+
+    def along_x(wave, zz, which, recv_sem):
         for k in (1, 3, 2):
-            send(at(wave, x, zz, which), send_sems.at[wave, 4 * i + k], recv_sem, (xs[k] * 8 + r % 8, c))
-
-    def along_z(wave, xx, i, which, send_sems, recv_sem):
+            send(at(wave, x, zz, which), recv_sem, (xs[k] * 8 + r % 8, c), wave)
+
+    def along_z(wave, xx, which, recv_sem):
         for k in (1, 3, 2):
-            device = (x * 8 + zs[k] * 2 + core, c)
-            send(at(wave, xx, zl, which), send_sems.at[wave, 4 * i + k], recv_sem, device)
-
-    def across(wave, xx, zz, which, n):
-        spot = 16 * n + xx * 4 + zz
-        send(at(wave, xx, zz, which), ssib.at[wave, spot], rsib.at[wave, spot], (sib, c))
+            send(at(wave, xx, zl, which), recv_sem, (x * 8 + zs[k] * 2 + core, c), wave)
+
+    def across(wave, xx, zz, which):
+        send(at(wave, xx, zz, which), sib_sem.at[wave], (sib, c), wave)
 
     def first_leg(wave):
-        along_z(wave, x, 0, lo, sza, rza.at[wave, zl])
-        along_x(wave, zl, 0, hi, sxb, rxb.at[wave, x])
-        along_x(wave, zl, 0, lo, sxa, rxa.at[wave, x * 4 + zl])
-        along_z(wave, x, 0, hi, szb, rzb.at[wave, x * 4 + zl])
-        across(wave, x, zl, lo, 0)
-        across(wave, x, zl, hi, 1)
+        along_z(wave, x, lo, line_sem.at[wave, zl])
+        along_x(wave, zl, hi, ring_sem.at[wave, x])
+        along_x(wave, zl, lo, group_sem.at[wave, 0])
+        along_z(wave, x, hi, group_sem.at[wave, 0])
+        across(wave, x, zl, whole)
 
     def second_leg(wave):
         for i in (1, 2, 3):
             xx = xs[nearest[i]]
-            got(at(wave, xx, zl, hi), rxb.at[wave, xx])
-            along_z(wave, xx, i, hi, szb, rzb.at[wave, xx * 4 + zl])
+            got(at(wave, xx, zl, hi), ring_sem.at[wave, xx])
+            along_z(wave, xx, hi, group_sem.at[wave, i])
             zz = order[i]
-            got(at(wave, x, zz, lo), rza.at[wave, zz])
-            along_x(wave, zz, i, lo, sxa, rxa.at[wave, x * 4 + zz])
-            across(wave, xx, zl, hi, 1)
-            across(wave, x, zz, lo, 0)
+            got(at(wave, x, zz, lo), line_sem.at[wave, zz])
+            along_x(wave, zz, lo, group_sem.at[wave, i])
+            across(wave, xx, zl, hi)
+            across(wave, x, zz, lo)
 
     def last_leg(wave):
         for i in range(4):
+            got(g_ref.at[wave, pl.ds(0, 3)], group_sem.at[wave, i])
             for k in (1, 2, 3):
-                zz, xx = order[i], xs[nearest[k]]
-                got(at(wave, xx, zz, lo), rxa.at[wave, xx * 4 + zz])
-                across(wave, xx, zz, lo, 0)
-                zz, xx = order[k], xs[nearest[i]]
-                got(at(wave, xx, zz, hi), rzb.at[wave, xx * 4 + zz])
-                across(wave, xx, zz, hi, 1)
-
-    for k in range(1, 8):
-        other = (me + k) % 8
-        got(recv1.at[0, other], rs1.at[other])
+                across(wave, xs[nearest[k]], order[i], lo)
+                across(wave, xs[nearest[i]], order[k], hi)
+
+    got(recv1.at[0, pl.ds(0, 7)], came1.at[0])
 
     @pl.when(core == 0)
     def _():
-        for k in range(1, 8):
-            other = (me + k) % 8
-            got(recv0.at[other], rs0.at[other])
+        got(recv0.at[pl.ds(0, 7)], came0)
 
     unpack(0)
     first_leg(0)
@@ -267,19 +259,18 @@
     def _():
         second_leg(0)
 
-    for k in range(8):
-        got(recv1.at[1, k], rs1.at[8 + k])
-
-        @pl.when(far_half == 0)
-        def _():
+    got(recv1.at[1], came1.at[1])
+
+    @pl.when(far_half == 0)
+    def _():
+        for k in range(8):
             far_piece(k).start()
-            if k >= 4:
-                far_lead(k - 4).start()
+        for k in range(4):
+            far_lead(k).start()
 
     @pl.when(core == 1)
     def _():
-        for k in range(8):
-            got(recv0.at[k], rs0.at[k])
+        got(recv0, came0)
 
     unpack(1)
     first_leg(1)
@@ -293,35 +284,18 @@
     last_leg(1)
 
     for wave in range(2):
-        for spot in range(16):
-            zz = spot % 4
-            b = (spot // 4) * 8 + (3 - zz if wave else zz) * 2 + 1 - core
-            got(g_ref.at[wave, b, lo], rsib.at[wave, spot])
-            got(g_ref.at[wave, b, hi], rsib.at[wave, 16 + spot])
+        got(g_ref.at[wave, pl.ds(0, 16)], sib_sem.at[wave])
 
     def left(ref, send_sem):
         remote(ref, ref, send_sem, load_sem.at[0], (sib, c)).wait_send()
 
     for wave in range(2):
-        small, large = g_ref.at[wave, 0, hi], g_ref.at[wave, 0, lo]
-        for k in (1, 2, 3):
-            left(large, sza.at[wave, k])
-            left(small, sxb.at[wave, k])
-            for i in range(4):
-                left(large, sxa.at[wave, 4 * i + k])
-                left(small, szb.at[wave, 4 * i + k])
-        for spot in range(16):
-            left(large, ssib.at[wave, spot])
-            left(small, ssib.at[wave, 16 + spot])
-    for k in range(8):
-        left(send1.at[1, k], ss1.at[8 + k])
-        if k:
-            left(send1.at[0, k], ss1.at[k])
-    for k in range(8):
-        if k:
-            left(send0, ss0.at[k])
-        else:
-            pl.when(core == 1)(near_lead(0).wait_send)
+        left(g_ref.at[wave, pl.ds(0, 31)], sent.at[wave])
+    left(send1.at[0, pl.ds(0, 7)], sent1.at[0])
+    left(send1.at[1], sent1.at[1])
+    left(recv0.at[pl.ds(0, 3)], sent0.at[0])
+    left(recv0.at[pl.ds(0, 4)], sent0.at[1])
+    pl.when(core == 1)(near_lead(0).wait_send)
     for load in loads[2:]:
         load.wait()
 
@@ -431,10 +405,8 @@
             pltpu.VMEM((16, 128), BF),
             pltpu.VMEM((8, 16, 128), BF),
             dma((6,)),
-            dma((16,)), dma((16,)), dma((8,)), dma((8,)),
-            dma((2, 4)), dma((2, 4)), dma((2, 16)), dma((2, 16)),
-            dma((2, 4)), dma((2, 4)), dma((2, 16)), dma((2, 16)),
-            dma((2, 32)), dma((2, 32)),
+            dma((2,)), dma((3,)), dma((2,)), dma(()),
+            dma((2,)), dma((2, 4)), dma((2, 4)), dma((2, 4)), dma((2,)),
         ],
         compiler_params=pltpu.CompilerParams(
             collective_id=0, has_side_effects=True, vmem_limit_bytes=32 << 20

time: 35.8 us -> 33 us (0.922)
  Pallas kernels: 35 us -> 32.2 us
    pallas_call x1, Pallas kernels: 31.5 us -> 28.7 us  [local(): pl.pallas_call(gather_kernel, out_shape=(pltpu.VMEM((2, ROWS, UNITS, 16,...]
where the time goes in v4:
time: 33 us; the launch traced here: 32.8 us
  Pallas kernels  32.2 us (98%)
  between operations  0.67 us (2%)
    pallas_call x1, Pallas kernels, local(): pl.pallas_call(gather_kernel, out_shape=(pltpu.VMEM((2, ROWS, UNITS, 16,...  28.7 us
    pallas_call x1, Pallas kernels, local(): pl.pallas_call(apply_kernel, out_shape=(jax.ShapeDtypeStruct(q_rows.shape...  3.47 us

profile of v4, /device:TPU:1, one launch (start us, length us, event | category | flops | bytes accessed | tf_op | source)
XLA Modules:
  0.0 32.8 jit_solution(6067917434948959193)
XLA Ops:
  0.6 0.0 copy-start
  0.6 0.0 copy-start.1
  0.7 28.7 %shard_map.102 = (bf16[2,32,9,16,128]{4,3,2,1,0:T(8,128)(2,1)S(1)}, bf16[128,8192]{1,0:T(8,128)(2,1)S(1)}, bf16[128,8192]{1,0:T(8,128)(2,1)S(1)}, bf16[256,256]{1,0:T(8,128)(2,1)S(1)}, bf16[256,256]{1,0:T(8,128)(2,1)S(1)}) custom-call(s32[16]{0:T(128)} %starts.1, bf16[16,2,8,32]{3,2,1,0:T(8,128)(2,1)} %factors_hbm.1, bf16[128,8192]{1,0:T(8,128)(2,1)} %q_hbm.1, ...), custom_call_target="tpu_custom_call" | custom-call | tf_op jit(solution)/shard_map/pallas_call | solution.py:388
  29.3 0.0 copy-done
  29.4 0.0 copy-done.1
  29.4 3.5 %shard_map.103 = (bf16[128,8192]{1,0:T(8,128)(2,1)}, bf16[128,8192]{1,0:T(8,128)(2,1)}, bf16[256,256]{1,0:T(8,128)(2,1)}, bf16[256,256]{1,0:T(8,128)(2,1)}) custom-call(s32[16]{0:T(128)S(1)} %copy-done, s32[16]{0:T(128)S(1)} %copy-done.1, bf16[128,8192]{1,0:T(8,128)(2,1)S(1)} %get-tuple-element.9.q, bf16[128,8192]{1,0:T(8,128)(2,1)S(1)} %get-tuple-element.10.z, ...), custom_call_target="tpu_custom_call" | custom-call | tf_op jit(solution)/shard_map/pallas_call | solution.py:418
Async XLA Ops:
  0.6 28.7 %copy-start = (s32[16]{0:T(128)S(1)}, s32[16]{0:T(128)}, u32[]{:S(2)}) copy-start(s32[16]{0:T(128)} %starts.1) | copy-start | bytes 196
  0.6 28.7 %copy-start.1 = (s32[16]{0:T(128)S(1)}, s32[16]{0:T(128)}, u32[]{:S(2)}) copy-start(s32[16]{0:T(128)} %flags.1) | copy-start | bytes 196

commit v5 on v4

--- a/solution.py
+++ b/solution.py
@@ -12,7 +12,9 @@
 ROWS = 32
 COLS = 8
 TILES = 32
-SPLIT = 7
+SPLITS = (7, 6)
+EARLY = 0
+PARTS = 4
 BF = jnp.bfloat16
 F32 = jnp.float32
 
@@ -37,10 +39,10 @@
 
 
 def gather_kernel(
-    starts_hbm, factors_hbm, q_hbm, z_hbm, s_hbm, t_hbm,
+    starts_hbm, factors_hbm, q_hbm, z_hbm, s_hbm, t_hbm, q_copied, z_copied,
     g_ref, qv, zv, sv, tv,
     starts_ref, fac, wide, send1, recv1, send0, recv0,
-    load_sem, sent1, sent0, came1, came0, sent, line_sem, ring_sem, group_sem, sib_sem,
+    load_sem, sent1, sent0, came1, came0, sent, line_sem, ring_sem, group_sem, sib_sem, far_sem,
 ):
     r = lax.axis_index("row")
     c = lax.axis_index("col")
@@ -75,12 +77,13 @@
         for k in range(8):
             greet((far_base + k // 4, far_col + k % 4))
 
-    for k in range(1, 8):
+    for k in (3, 1, 2):
+        greet((x * 8 + (zl + k) % 4 * 2 + core, c))
+    for k in (4, 2, 6, 5, 3, 1, 7):
         other = (me + k) % 8
         greet((near_base + other // 4, near_col + other % 4))
-    for k in range(1, 4):
+    for k in (2, 1, 3):
         greet(((r + 8 * k) % ROWS, c))
-        greet((x * 8 + (zl + k) % 4 * 2 + core, c))
 
     wide[...] = jnp.zeros_like(wide)
     loads[0].wait()
@@ -139,6 +142,13 @@
     def _():
         pl.semaphore_wait(barrier, 21)
         for k in range(8):
+            pl.semaphore_signal(
+                far_sem,
+                inc=1,
+                device_id=(far_base + k // 4, far_col + k % 4),
+                device_id_type=pl.DeviceIdType.MESH,
+            )
+        for k in range(8):
             far_piece(k).start()
         for k in range(4):
             far_lead(k).start()
@@ -197,15 +207,14 @@
         jnp.where(zl < 2, 2, jnp.where(zl == 2, 3, 1)),
         jnp.where(zl < 2, 3, 0),
     ]
-    lo = pl.ds(0, SPLIT)
-    hi = pl.ds(SPLIT, UNITS - SPLIT)
-    whole = pl.ds(0, UNITS)
+    lo, hi, whole = (0, 1, 2)
+    spans = [(pl.ds(0, n), pl.ds(n, UNITS - n), pl.ds(0, UNITS)) for n in SPLITS]
     xs = [(x + k) % 4 for k in range(4)]
     zs = [(zl + k) % 4 for k in range(4)]
     nearest = (0, 1, 3, 2)
 
     def at(wave, xx, zz, which):
-        return g_ref.at[wave, xx * 8 + (3 - zz if wave else zz) * 2 + core, which]
+        return g_ref.at[wave, xx * 8 + (3 - zz if wave else zz) * 2 + core, spans[wave][which]]
 
     def send(ref, recv_sem, device, wave):
         remote(ref, ref, sent.at[wave], recv_sem, device).start()
@@ -255,29 +264,23 @@
     unpack(0)
     first_leg(0)
 
-    @pl.when(far_half == 1)
-    def _():
-        second_leg(0)
-
-    got(recv1.at[1], came1.at[1])
-
     @pl.when(far_half == 0)
     def _():
+        pl.semaphore_wait(far_sem, 8)
         for k in range(8):
             far_piece(k).start()
         for k in range(4):
             far_lead(k).start()
 
+    second_leg(0)
+    got(recv1.at[1], came1.at[1])
+
     @pl.when(core == 1)
     def _():
         got(recv0, came0)
 
     unpack(1)
     first_leg(1)
-
-    @pl.when(far_half == 0)
-    def _():
-        second_leg(0)
 
     second_leg(1)
     last_leg(0)
@@ -300,8 +303,32 @@
         load.wait()
 
 
+def early():
+    r, c = lax.axis_index("row"), lax.axis_index("col")
+    return jnp.logical_and(c < 4, 2 * (r // 8) + 2 * c + 3 * ((r // 2) % 4) <= EARLY)
+
+
+def copy_kernel(q, z, q_out, z_out, held, in_sem, out_sem):
+    @pl.when(early())
+    def _():
+        ins, outs = [], []
+        for i in range(PARTS):
+            part = pl.ds(128 // PARTS * i, 128 // PARTS)
+            for n, (src, dst) in enumerate(((q, q_out), (z, z_out))):
+                spot = 2 * i + n
+                ins.append(pltpu.make_async_copy(src.at[part], held.at[n, part], in_sem.at[spot]))
+                outs.append(pltpu.make_async_copy(held.at[n, part], dst.at[part], out_sem.at[spot]))
+        for copy in ins:
+            copy.start()
+        for arrive, leave in zip(ins, outs):
+            arrive.wait()
+            leave.start()
+        for copy in outs:
+            copy.wait()
+
+
 def apply_kernel(
-    starts, flags, q, z, s, t, g, q_out, z_out, s_out, t_out, q_new, z_new, band, q_sem, z_sem, b_sem, whole_sem
+    starts, flags, q, z, s, t, g, q_copied, z_copied, q_out, z_out, s_out, t_out, q_new, z_new, band, q_sem, z_sem, b_sem, whole_sem
 ):
     r = lax.axis_index("row")
     c = lax.axis_index("col")
@@ -316,7 +343,7 @@
 
     wholes = [pltpu.make_async_copy(q, q_out, whole_sem.at[0]), pltpu.make_async_copy(z, z_out, whole_sem.at[1])]
     for whole in wholes:
-        whole.start()
+        pl.when(jnp.logical_not(early()))(whole.start)
 
     def q_copy(j, tile):
         return pltpu.make_async_copy(q_new.at[j], q_out.at[:, pl.ds(pl.multiple_of(tile * W, W), W)], q_sem.at[j])
@@ -361,7 +388,7 @@
         copy.start()
         outs.append(copy)
     for whole in wholes:
-        whole.wait()
+        pl.when(jnp.logical_not(early()))(whole.wait)
     for j, (live, tile) in enumerate(slots):
 
         @pl.when(live)
@@ -385,6 +412,17 @@
     vmem = pl.BlockSpec(memory_space=pltpu.VMEM)
     smem = pl.BlockSpec(memory_space=pltpu.SMEM)
     dma = pltpu.SemaphoreType.DMA
+    copied = pl.pallas_call(
+        copy_kernel,
+        out_shape=(
+            jax.ShapeDtypeStruct(q_rows.shape, BF),
+            jax.ShapeDtypeStruct(z_rows.shape, BF),
+        ),
+        in_specs=[hbm] * 2,
+        out_specs=[hbm] * 2,
+        scratch_shapes=[pltpu.VMEM((2, *q_rows.shape), BF), dma((2 * PARTS,)), dma((2 * PARTS,))],
+        compiler_params=pltpu.CompilerParams(vmem_limit_bytes=32 << 20),
+    )(*(pltpu.with_memory_space_constraint(a, pltpu.HBM) for a in (q_rows, z_rows)))
     gathered, qv, zv, sv, tv = pl.pallas_call(
         gather_kernel,
         out_shape=(
@@ -394,7 +432,7 @@
             pltpu.VMEM(s_band.shape, BF),
             pltpu.VMEM(t_band.shape, BF),
         ),
-        in_specs=[hbm] * 6,
+        in_specs=[hbm] * 8,
         out_specs=[vmem] * 5,
         scratch_shapes=[
             pltpu.SMEM((K,), jnp.int32),
@@ -407,11 +445,12 @@
             dma((6,)),
             dma((2,)), dma((3,)), dma((2,)), dma(()),
             dma((2,)), dma((2, 4)), dma((2, 4)), dma((2, 4)), dma((2,)),
+            pltpu.SemaphoreType.REGULAR,
         ],
         compiler_params=pltpu.CompilerParams(
             collective_id=0, has_side_effects=True, vmem_limit_bytes=32 << 20
         ),
-    )(*(pltpu.with_memory_space_constraint(a, pltpu.HBM) for a in (starts, factors, q_rows, z_rows, s_band, t_band)))
+    )(*(pltpu.with_memory_space_constraint(a, pltpu.HBM) for a in (starts, factors, q_rows, z_rows, s_band, t_band, *copied)))
     gathered = gathered.reshape(2, 16, 2, UNITS, 16, 128)
     pin = lambda a: pltpu.with_memory_space_constraint(a, pltpu.VMEM)
     return tuple(
@@ -423,8 +462,9 @@
                 jax.ShapeDtypeStruct(s_band.shape, BF),
                 jax.ShapeDtypeStruct(t_band.shape, BF),
             ),
-            in_specs=[smem, smem] + [vmem] * 5,
-            out_specs=[anywhere] * 4,
+            in_specs=[smem, smem] + [vmem] * 5 + [hbm] * 2,
+            out_specs=[hbm] * 2 + [anywhere] * 2,
+            input_output_aliases={7: 0, 8: 1},
             scratch_shapes=[
                 pltpu.VMEM((SLOTS, 128, W), BF),
                 pltpu.VMEM((SLOTS, 128, W), BF),
@@ -435,7 +475,7 @@
                 dma((2,)),
             ],
             compiler_params=pltpu.CompilerParams(vmem_limit_bytes=32 << 20),
-        )(starts, flags, *(pin(a) for a in (qv, zv, sv, tv, gathered)))
+        )(starts, flags, *(pin(a) for a in (qv, zv, sv, tv, gathered)), *(pltpu.with_memory_space_constraint(a, pltpu.HBM) for a in copied))
     )
 
 

time: 33 us -> 32.3 us (0.979)
  Pallas kernels: 32.2 us -> 31.4 us
    pallas_call x0 -> x1, Pallas kernels: none -> 3.6 us  [local(): pl.pallas_call(copy_kernel, out_shape=(jax.ShapeDtypeStruct(q_rows.shape,...]
    pallas_call x1, Pallas kernels: 28.7 us -> 25.3 us  [local(): pl.pallas_call(gather_kernel, out_shape=(pltpu.VMEM((2, ROWS, UNITS, 16,...]
    pallas_call x1, Pallas kernels: 3.47 us -> 2.51 us  [local(): pl.pallas_call(apply_kernel, out_shape=(jax.ShapeDtypeStruct(q_rows.shape...]
where the time goes in v5:
time: 32.3 us; the launch traced here: 32.1 us
  Pallas kernels  31.4 us (97%)
  between operations  0.68 us (2%)
    pallas_call x1, Pallas kernels, local(): pl.pallas_call(gather_kernel, out_shape=(pltpu.VMEM((2, ROWS, UNITS, 16,...  25.3 us
    pallas_call x1, Pallas kernels, local(): pl.pallas_call(copy_kernel, out_shape=(jax.ShapeDtypeStruct(q_rows.shape,...  3.6 us
    pallas_call x1, Pallas kernels, local(): pl.pallas_call(apply_kernel, out_shape=(jax.ShapeDtypeStruct(q_rows.shape...  2.51 us

profile of v5, /device:TPU:1, one launch (start us, length us, event | category | flops | bytes accessed | tf_op | source)
XLA Modules:
  0.0 32.1 jit_solution(16001227055771415533)
XLA Ops:
  0.6 3.6 %shard_map.102 = (bf16[128,8192]{1,0:T(8,128)(2,1)}, bf16[128,8192]{1,0:T(8,128)(2,1)}) custom-call(bf16[128,8192]{1,0:T(8,128)(2,1)} %q_hbm.1, bf16[128,8192]{1,0:T(8,128)(2,1)} %z_hbm.1), custom_call_target="tpu_custom_call" | custom-call | tf_op jit(solution)/shard_map/pallas_call | solution.py:415
  4.2 0.0 copy-start
  4.3 0.0 copy-start.1
  4.3 25.3 %shard_map.103 = (bf16[2,32,9,16,128]{4,3,2,1,0:T(8,128)(2,1)S(1)}, bf16[128,8192]{1,0:T(8,128)(2,1)S(1)}, bf16[128,8192]{1,0:T(8,128)(2,1)S(1)}, bf16[256,256]{1,0:T(8,128)(2,1)S(1)}, bf16[256,256]{1,0:T(8,128)(2,1)S(1)}) custom-call(s32[16]{0:T(128)} %starts.1, bf16[16,2,8,32]{3,2,1,0:T(8,128)(2,1)} %factors_hbm.1, bf16[128,8192]{1,0:T(8,128)(2,1)} %q_hbm.1, ...), custom_call_target="tpu_custom_call" | custom-call | tf_op jit(solution)/shard_map/pallas_call | solution.py:426
  29.6 0.0 copy-done
  29.6 0.0 copy-done.1
  29.6 2.5 %shard_map.104 = (bf16[128,8192]{1,0:T(8,128)(2,1)}, bf16[128,8192]{1,0:T(8,128)(2,1)}, bf16[256,256]{1,0:T(8,128)(2,1)}, bf16[256,256]{1,0:T(8,128)(2,1)}) custom-call(s32[16]{0:T(128)S(1)} %copy-done, s32[16]{0:T(128)S(1)} %copy-done.1, bf16[128,8192]{1,0:T(8,128)(2,1)S(1)} %get-tuple-element.13.q, ...), custom_call_target="tpu_custom_call", output_to_operand_aliasing={{0}: (7, {}), {1}: (8, {})} | custom-call | tf_op jit(solution)/shard_map/pallas_call | solution.py:457
Async XLA Ops:
  4.2 25.4 %copy-start = (s32[16]{0:T(128)S(1)}, s32[16]{0:T(128)}, u32[]{:S(2)}) copy-start(s32[16]{0:T(128)} %starts.1) | copy-start | bytes 196
  4.3 25.4 %copy-start.1 = (s32[16]{0:T(128)S(1)}, s32[16]{0:T(128)}, u32[]{:S(2)}) copy-start(s32[16]{0:T(128)} %flags.1) | copy-start | bytes 196

commit v6 on v5

--- a/solution.py
+++ b/solution.py
@@ -12,8 +12,8 @@
 ROWS = 32
 COLS = 8
 TILES = 32
-SPLITS = (7, 6)
-EARLY = 0
+SPLITS = (7, 5)
+EARLY = 2
 PARTS = 4
 BF = jnp.bfloat16
 F32 = jnp.float32
@@ -39,9 +39,9 @@
 
 
 def gather_kernel(
-    starts_hbm, factors_hbm, q_hbm, z_hbm, s_hbm, t_hbm, q_copied, z_copied,
-    g_ref, qv, zv, sv, tv,
-    starts_ref, fac, wide, send1, recv1, send0, recv0,
+    starts_hbm, flags_hbm, factors_hbm, q_hbm, z_hbm, s_hbm, t_hbm, q_copied, z_copied,
+    g_ref, qv, zv, sv, tv, starts_ref, flags_ref,
+    fac, wide, send1, recv1, send0, recv0,
     load_sem, sent1, sent0, came1, came0, sent, line_sem, ring_sem, group_sem, sib_sem, far_sem,
 ):
     r = lax.axis_index("row")
@@ -66,7 +66,7 @@
     loads = [
         pltpu.make_async_copy(a, b, load_sem.at[i])
         for i, (a, b) in enumerate(
-            [(factors_hbm, fac), (starts_hbm, starts_ref), (q_hbm, qv), (z_hbm, zv), (s_hbm, sv), (t_hbm, tv)]
+            [(factors_hbm, fac), (starts_hbm, starts_ref), (q_hbm, qv), (z_hbm, zv), (s_hbm, sv), (t_hbm, tv), (flags_hbm, flags_ref)]
         )
     ]
     loads[0].start()
@@ -332,6 +332,10 @@
 ):
     r = lax.axis_index("row")
     c = lax.axis_index("col")
+    wholes = [pltpu.make_async_copy(q, q_out, whole_sem.at[0]), pltpu.make_async_copy(z, z_out, whole_sem.at[1])]
+    for whole in wholes:
+        pl.when(jnp.logical_not(early()))(whole.start)
+
     word = slot_words(starts, c)
     count = jnp.int32(0)
     windows = jnp.int32(0)
@@ -340,10 +344,6 @@
         count = count + jnp.where(mine, 1, 0)
         bit = jnp.left_shift(jnp.int32(1), (starts[k] >> 8) & (TILES - 1))
         windows = jnp.where(jnp.logical_and(mine, flags[k] == 1), windows | bit, windows)
-
-    wholes = [pltpu.make_async_copy(q, q_out, whole_sem.at[0]), pltpu.make_async_copy(z, z_out, whole_sem.at[1])]
-    for whole in wholes:
-        pl.when(jnp.logical_not(early()))(whole.start)
 
     def q_copy(j, tile):
         return pltpu.make_async_copy(q_new.at[j], q_out.at[:, pl.ds(pl.multiple_of(tile * W, W), W)], q_sem.at[j])
@@ -387,14 +387,10 @@
         copy = pltpu.make_async_copy(band.at[i], out, b_sem.at[i])
         copy.start()
         outs.append(copy)
-    for whole in wholes:
+    for whole, new_copy in zip(wholes, (q_copy, z_copy)):
         pl.when(jnp.logical_not(early()))(whole.wait)
-    for j, (live, tile) in enumerate(slots):
-
-        @pl.when(live)
-        def _():
-            q_copy(j, tile).start()
-            z_copy(j, tile).start()
+        for j, (live, tile) in enumerate(slots):
+            pl.when(live)(new_copy(j, tile).start)
 
     for copy in outs:
         copy.wait()
@@ -423,7 +419,7 @@
         scratch_shapes=[pltpu.VMEM((2, *q_rows.shape), BF), dma((2 * PARTS,)), dma((2 * PARTS,))],
         compiler_params=pltpu.CompilerParams(vmem_limit_bytes=32 << 20),
     )(*(pltpu.with_memory_space_constraint(a, pltpu.HBM) for a in (q_rows, z_rows)))
-    gathered, qv, zv, sv, tv = pl.pallas_call(
+    gathered, qv, zv, sv, tv, starts_held, flags_held = pl.pallas_call(
         gather_kernel,
         out_shape=(
             pltpu.VMEM((2, ROWS, UNITS, 16, 128), BF),
@@ -431,18 +427,19 @@
             pltpu.VMEM(z_rows.shape, BF),
             pltpu.VMEM(s_band.shape, BF),
             pltpu.VMEM(t_band.shape, BF),
+            pltpu.SMEM((K,), jnp.int32),
+            pltpu.SMEM((K,), jnp.int32),
         ),
-        in_specs=[hbm] * 8,
-        out_specs=[vmem] * 5,
+        in_specs=[hbm] * 9,
+        out_specs=[vmem] * 5 + [smem] * 2,
         scratch_shapes=[
-            pltpu.SMEM((K,), jnp.int32),
             pltpu.VMEM((K, 2, 8, 32), BF),
             pltpu.VMEM((K, 16, 128), F32),
             pltpu.VMEM((2, 8, 16, 128), BF),
             pltpu.VMEM((2, 8, 16, 128), BF),
             pltpu.VMEM((16, 128), BF),
             pltpu.VMEM((8, 16, 128), BF),
-            dma((6,)),
+            dma((7,)),
             dma((2,)), dma((3,)), dma((2,)), dma(()),
             dma((2,)), dma((2, 4)), dma((2, 4)), dma((2, 4)), dma((2,)),
             pltpu.SemaphoreType.REGULAR,
@@ -450,7 +447,7 @@
         compiler_params=pltpu.CompilerParams(
             collective_id=0, has_side_effects=True, vmem_limit_bytes=32 << 20
         ),
-    )(*(pltpu.with_memory_space_constraint(a, pltpu.HBM) for a in (starts, factors, q_rows, z_rows, s_band, t_band, *copied)))
+    )(*(pltpu.with_memory_space_constraint(a, pltpu.HBM) for a in (starts, flags, factors, q_rows, z_rows, s_band, t_band, *copied)))
     gathered = gathered.reshape(2, 16, 2, UNITS, 16, 128)
     pin = lambda a: pltpu.with_memory_space_constraint(a, pltpu.VMEM)
     return tuple(
@@ -475,7 +472,7 @@
                 dma((2,)),
             ],
             compiler_params=pltpu.CompilerParams(vmem_limit_bytes=32 << 20),
-        )(starts, flags, *(pin(a) for a in (qv, zv, sv, tv, gathered)), *(pltpu.with_memory_space_constraint(a, pltpu.HBM) for a in copied))
+        )(*(pltpu.with_memory_space_constraint(a, pltpu.SMEM) for a in (starts_held, flags_held)), *(pin(a) for a in (qv, zv, sv, tv, gathered)), *(pltpu.with_memory_space_constraint(a, pltpu.HBM) for a in copied))
     )
 
 

time: 32.3 us -> 32.6 us (level)
  Pallas kernels: 31.4 us -> 31.8 us
    pallas_call x1, Pallas kernels: 2.51 us -> 3.14 us  [local(): pl.pallas_call(apply_kernel, out_shape=(jax.ShapeDtypeStruct(q_rows.shape...]
where the time goes in v6:
time: 32.6 us; the launch traced here: 32.5 us
  Pallas kernels  31.8 us (98%)
  between operations  0.65 us (2%)
    pallas_call x1, Pallas kernels, local(): pl.pallas_call(gather_kernel, out_shape=(pltpu.VMEM((2, ROWS, UNITS, 16,...  25.1 us
    pallas_call x1, Pallas kernels, local(): pl.pallas_call(copy_kernel, out_shape=(jax.ShapeDtypeStruct(q_rows.shape,...  3.6 us
    pallas_call x1, Pallas kernels, local(): pl.pallas_call(apply_kernel, out_shape=(jax.ShapeDtypeStruct(q_rows.shape...  3.14 us

profile of v6, /device:TPU:1, one launch (start us, length us, event | category | flops | bytes accessed | tf_op | source)
XLA Modules:
  0.0 32.5 jit_solution(13975217974753018248)
XLA Ops:
  0.6 3.6 %shard_map.102 = (bf16[128,8192]{1,0:T(8,128)(2,1)}, bf16[128,8192]{1,0:T(8,128)(2,1)}) custom-call(bf16[128,8192]{1,0:T(8,128)(2,1)} %q_hbm.1, bf16[128,8192]{1,0:T(8,128)(2,1)} %z_hbm.1), custom_call_target="tpu_custom_call" | custom-call | tf_op jit(solution)/shard_map/pallas_call | solution.py:411
  4.2 25.1 %shard_map.103 = (bf16[2,32,9,16,128]{4,3,2,1,0:T(8,128)(2,1)S(1)}, bf16[128,8192]{1,0:T(8,128)(2,1)S(1)}, bf16[128,8192]{1,0:T(8,128)(2,1)S(1)}, bf16[256,256]{...) custom-call(s32[16]{0:T(128)} %starts_hbm.1, s32[16]{0:T(128)} %flags_hbm.1, ...), custom_call_target="tpu_custom_call" | custom-call | tf_op jit(solution)/shard_map/pallas_call | solution.py:422
  29.3 3.1 %shard_map.104 = (bf16[128,8192]{1,0:T(8,128)(2,1)}, bf16[128,8192]{1,0:T(8,128)(2,1)}, bf16[256,256]{1,0:T(8,128)(2,1)}, bf16[256,256]{1,0:T(8,128)(2,1)}) custom-call(s32[16]{0:T(128)S(4)} %get-tuple-element.15.starts, s32[16]{0:T(128)S(4)} %get-tuple-element.16.flags, ...), custom_call_target="tpu_custom_call", output_to_operand_aliasing={{0}: (7, {}), {1}: (8, {})} | custom-call | tf_op jit(solution)/shard_map/pallas_call | solution.py:454

commit v7 on v6

--- a/solution.py
+++ b/solution.py
@@ -13,7 +13,7 @@
 COLS = 8
 TILES = 32
 SPLITS = (7, 5)
-EARLY = 2
+EARLY = 4
 PARTS = 4
 BF = jnp.bfloat16
 F32 = jnp.float32
@@ -366,11 +366,18 @@
         band_slot = jnp.where(jnp.logical_and(j < count, tile == r), j, band_slot)
         slots.append((live, tile))
 
-        @pl.when(live)
-        def _():
-            where = pl.ds(pl.multiple_of(tile * W, W), W)
-            q_new[j] = jnp.dot(q[:, where], factor(0, j), preferred_element_type=F32).astype(BF)
-            z_new[j] = jnp.dot(z[:, where], factor(1, j), preferred_element_type=F32).astype(BF)
+        where = pl.ds(pl.multiple_of(tile * W, W), W)
+        q_new[j] = jnp.dot(q[:, where], factor(0, j), preferred_element_type=F32).astype(BF)
+        z_new[j] = jnp.dot(z[:, where], factor(1, j), preferred_element_type=F32).astype(BF)
+
+        if j % 2 == 1:
+            for jj in range(j - 1, j + 1):
+                live, tile = slots[jj]
+
+                @pl.when(jnp.logical_and(live, early()))
+                def _():
+                    q_copy(jj, tile).start()
+                    z_copy(jj, tile).start()
 
     band_live = ((windows >> r) & 1) == 1
     right = factor(1, band_slot)
@@ -390,7 +397,7 @@
     for whole, new_copy in zip(wholes, (q_copy, z_copy)):
         pl.when(jnp.logical_not(early()))(whole.wait)
         for j, (live, tile) in enumerate(slots):
-            pl.when(live)(new_copy(j, tile).start)
+            pl.when(jnp.logical_and(live, jnp.logical_not(early())))(new_copy(j, tile).start)
 
     for copy in outs:
         copy.wait()

time: 32.6 us -> 31.1 us (0.954)
  Pallas kernels: 31.8 us -> 30.4 us
    pallas_call x1, Pallas kernels: 3.14 us -> 1.67 us  [local(): pl.pallas_call(apply_kernel, out_shape=(jax.ShapeDtypeStruct(q_rows.shape...]
where the time goes in v7:
time: 31.1 us; the launch traced here: 31 us
  Pallas kernels  30.4 us (98%)
  between operations  0.65 us (2%)
    pallas_call x1, Pallas kernels, local(): pl.pallas_call(gather_kernel, out_shape=(pltpu.VMEM((2, ROWS, UNITS, 16,...  25.1 us
    pallas_call x1, Pallas kernels, local(): pl.pallas_call(copy_kernel, out_shape=(jax.ShapeDtypeStruct(q_rows.shape,...  3.6 us
    pallas_call x1, Pallas kernels, local(): pl.pallas_call(apply_kernel, out_shape=(jax.ShapeDtypeStruct(q_rows.shape...  1.67 us

profile of v7, /device:TPU:1, one launch (start us, length us, event | category | flops | bytes accessed | tf_op | source)
XLA Modules:
  0.0 31.0 jit_solution(3886263077340942581)
XLA Ops:
  0.6 3.6 %shard_map.102 = (bf16[128,8192]{1,0:T(8,128)(2,1)}, bf16[128,8192]{1,0:T(8,128)(2,1)}) custom-call(bf16[128,8192]{1,0:T(8,128)(2,1)} %q_hbm.1, bf16[128,8192]{1,0:T(8,128)(2,1)} %z_hbm.1), custom_call_target="tpu_custom_call" | custom-call | tf_op jit(solution)/shard_map/pallas_call | solution.py:418
  4.2 25.1 %shard_map.103 = (bf16[2,32,9,16,128]{4,3,2,1,0:T(8,128)(2,1)S(1)}, bf16[128,8192]{1,0:T(8,128)(2,1)S(1)}, bf16[128,8192]{1,0:T(8,128)(2,1)S(1)}, bf16[256,256]{...) custom-call(s32[16]{0:T(128)} %starts_hbm.1, s32[16]{0:T(128)} %flags_hbm.1, ...), custom_call_target="tpu_custom_call" | custom-call | tf_op jit(solution)/shard_map/pallas_call | solution.py:429
  29.3 1.7 %shard_map.104 = (bf16[128,8192]{1,0:T(8,128)(2,1)}, bf16[128,8192]{1,0:T(8,128)(2,1)}, bf16[256,256]{1,0:T(8,128)(2,1)}, bf16[256,256]{1,0:T(8,128)(2,1)}) custom-call(s32[16]{0:T(128)S(4)} %get-tuple-element.15.starts, s32[16]{0:T(128)S(4)} %get-tuple-element.16.flags, ...), custom_call_target="tpu_custom_call", output_to_operand_aliasing={{0}: (7, {}), {1}: (8, {})} | custom-call | tf_op jit(solution)/shard_map/pallas_call | solution.py:461
